TPU v7x, 32 devices: a whole 2x2x4 slice. The times are simulated.
32 devices in a mesh: section: 2 (over core), req: 16 (over z, y, x).
Axes of the slice: x: 2, y: 2, z: 4, core: 2. Of those that a mesh axis runs over, the one named last changes fastest.
Arguments:
- section_in: bfloat16 [2, 16, 32, 1152], P('section', 'req'), may hold values from -24 to 24
- patch_index: int32 [2, 16], P('section', 'req'), may hold values from 0 to 3
- stale_kv: bfloat16 [2, 16, 128, 2304], P('section', 'req'), may hold values from -400 to 400
- modulation: float32 [2, 16, 6, 1152], P('section', 'req'), may hold values from -4 to 4
- final_mod: float32 [16, 2, 1152], P('req'), may hold values from -4 to 4
- qkv_blocks: bfloat16 [2, 16, 1152, 864], P('section', 'req'), may hold values from -1 to 1, as said below
- out_blocks: bfloat16 [2, 16, 1152, 288], P('section', 'req'), may hold values from -1 to 1, as said below
- up_blocks: bfloat16 [2, 16, 1152, 1152], P('section', 'req'), may hold values from -1 to 1, as said below
- down_blocks: bfloat16 [2, 16, 1152, 1152], P('section', 'req'), may hold values from -1 to 1, as said below
- final_weight: bfloat16 [1152, 16], replicated, may hold values from -0.1875 to 0.1875
- noisy_latent: float32 [16, 512], P('req', 'section'), may hold values from -6 to 6
- time_index: int32 [16], P('req'), may hold values from 100 to 499
- time_gap: int32 [16], P('req'), may hold values from 10 to 40
Outputs:
- fresh_kv: bfloat16 [2, 16, 32, 2304], P('section', 'req')
- next_input: bfloat16 [16, 32, 1152], P('req', 'section')
- noise_pred: float32 [16, 512], P('req', 'section')
- denoised: float32 [16, 512], P('req', 'section')
Inputs may be any that keep to these rules, and one draw needn't show every extreme that they name: qkv_blocks[s, r] equals qkv_blocks[s, r mod 4]. out_blocks[s, r] equals out_blocks[s, r mod 4]. up_blocks[s, r] equals up_blocks[s, r mod 4]. down_blocks[s, r] equals down_blocks[s, r mod 4].
All inputs are finite; a program needn't handle non-finite values.
Results may differ from a plain program's by a relative error of at most 0.0093.
Values may be sent and summed in bfloat16 or wider, within the bound.
No kernel may reach another device: no remote copies, remote signals or barrier semaphores. Data moves between devices by JAX's collectives and lax.ppermute only.
A program may use at most 64 MiB of HBM per device.

v0:
```python
from functools import partial

import jax
import jax.numpy as jnp
from jax import lax
from jax.sharding import PartitionSpec as P

HEADS = 16
UNIT_GROUPS = 4


NORM_EPS = 1e-06
BETA_LOW = 0.0001
BETA_HIGH = 0.02


def from_partner(x, axis, bit):
    return lax.ppermute(x, axis, [(i, i ^ 1 << bit) for i in range(lax.axis_size(axis))])


def layer_norm(values):
    average = jnp.mean(values, axis=-1, keepdims=True)
    centred = values - average
    spread = jnp.mean(centred * centred, axis=-1, keepdims=True)
    return centred * lax.rsqrt(spread + NORM_EPS)


def alpha_bar(step_index):
    moment = step_index.astype(jnp.float32)
    return jnp.exp(
        -(BETA_LOW * (moment + 1.0) + (BETA_HIGH - BETA_LOW) * moment * (moment + 1.0) / 1998.0)
    )


def attend(queries, fresh_keys, fresh_values, stale_rows, patch_at):
    fresh_count = queries.shape[0]
    model_width = queries.shape[1]
    head_size = model_width // HEADS
    fresh_rows = jnp.concatenate([fresh_keys, fresh_values], axis=1)
    start = patch_at * fresh_count
    all_rows = lax.dynamic_update_slice(stale_rows, fresh_rows, (start, jnp.zeros((), jnp.int32)))
    key_rows = all_rows[:, :model_width]
    value_rows = all_rows[:, model_width:]
    scores = jnp.einsum(
        "qhd,khd->hqk",
        queries.reshape(fresh_count, HEADS, head_size),
        key_rows.reshape(-1, HEADS, head_size),
        preferred_element_type=jnp.float32,
    ) * head_size ** (-0.5)
    highest = jnp.max(scores, axis=-1, keepdims=True)
    raised = jnp.exp(scores - highest)
    attention_weights = (raised / jnp.sum(raised, axis=-1, keepdims=True)).astype(jnp.bfloat16)
    mixed = jnp.einsum(
        "hqk,khd->qhd",
        attention_weights,
        value_rows.reshape(-1, HEADS, head_size),
        preferred_element_type=jnp.float32,
    )
    return mixed.reshape(fresh_count, model_width).astype(jnp.bfloat16)


def block_product(incoming, weight):
    return jnp.einsum("nsd,dc->nsc", incoming, weight, preferred_element_type=jnp.float32).astype(
        jnp.bfloat16
    )


def unit_block(incoming, w_up, w_down):
    inner = jax.nn.gelu(
        jnp.einsum("nsd,df->nsf", incoming, w_up, preferred_element_type=jnp.float32),
        approximate=True,
    ).astype(jnp.bfloat16)
    return jnp.einsum("nsf,fd->nsd", inner, w_down, preferred_element_type=jnp.float32).astype(
        jnp.bfloat16
    )


def spread_regroup(token_rows, block_fn, staggered):
    devices = lax.axis_size("req")
    slices = devices // UNIT_GROUPS
    feature = token_rows.shape[1]
    per_slice = token_rows.shape[0] // slices
    pieces = token_rows.reshape(slices, per_slice, feature)
    outgoing = jnp.broadcast_to(pieces[:, None], (slices, UNIT_GROUPS, per_slice, feature)).reshape(
        devices, per_slice, feature
    )
    returned = lax.all_to_all(
        block_fn(lax.all_to_all(outgoing, "req", split_axis=0, concat_axis=0, tiled=True)),
        "req",
        split_axis=0,
        concat_axis=0,
        tiled=True,
    )
    columns = returned.shape[-1]
    ordered = returned.reshape(slices, UNIT_GROUPS, per_slice, columns).transpose(0, 2, 1, 3)
    return ordered.reshape(slices * per_slice, UNIT_GROUPS, columns)


def layer_step(hidden, stale_rows, mods, patch_at, w_qkv, w_out, w_up, w_down, regroup):
    fresh_count = hidden.shape[0]
    model_width = hidden.shape[1]
    residual = hidden.astype(jnp.float32)
    normed = (layer_norm(residual) * (1.0 + mods[1]) + mods[0]).astype(jnp.bfloat16)
    joined = regroup(normed, partial(block_product, weight=w_qkv))
    joined = joined.reshape(fresh_count, UNIT_GROUPS, 3, model_width // UNIT_GROUPS)
    queries = joined[:, :, 0].reshape(fresh_count, model_width)
    fresh_keys = joined[:, :, 1].reshape(fresh_count, model_width)
    fresh_values = joined[:, :, 2].reshape(fresh_count, model_width)
    mixed = attend(queries, fresh_keys, fresh_values, stale_rows, patch_at)
    projected = regroup(mixed, partial(block_product, weight=w_out)).reshape(
        fresh_count, model_width
    )
    after_attention = residual + mods[2] * projected.astype(jnp.float32)
    middle = (layer_norm(after_attention) * (1.0 + mods[4]) + mods[3]).astype(jnp.bfloat16)
    parts = regroup(middle, partial(unit_block, w_up=w_up, w_down=w_down))
    total = jnp.sum(parts.astype(jnp.float32), axis=1)
    layer_out = (after_attention + mods[5] * total).astype(jnp.bfloat16)
    return (layer_out, jnp.concatenate([fresh_keys, fresh_values], axis=1))


def per_device(
    section_in,
    patch_index,
    stale_kv,
    modulation,
    final_mod,
    qkv_blocks,
    out_blocks,
    up_blocks,
    down_blocks,
    final_weight,
    noisy_latent,
    time_index,
    time_gap,
):
    regroup = partial(spread_regroup, staggered=False)
    hidden = section_in[0, 0]
    layer_out, fresh = layer_step(
        hidden,
        stale_kv[0, 0],
        modulation[0, 0],
        patch_index[0, 0],
        qkv_blocks[0, 0],
        out_blocks[0, 0],
        up_blocks[0, 0],
        down_blocks[0, 0],
        regroup,
    )
    half_rows = hidden.shape[0] // 2
    upper = layer_out[:half_rows]
    lower = layer_out[half_rows:]
    section_id = lax.axis_index("section")
    leaving = jnp.where(section_id == 0, lower, upper)
    arrived = from_partner(leaving, "section", 0)
    next_rows = jnp.where(section_id == 0, upper, arrived)
    final_rows = jnp.where(section_id == 0, arrived, lower)
    shifted = (
        layer_norm(final_rows.astype(jnp.float32)) * (1.0 + final_mod[0, 1]) + final_mod[0, 0]
    ).astype(jnp.bfloat16)
    noise_pred = jnp.dot(shifted, final_weight, preferred_element_type=jnp.float32).reshape(1, -1)
    now_bar = alpha_bar(time_index[0])
    prev_bar = alpha_bar(time_index[0] - time_gap[0])
    clean_latent = (noisy_latent - jnp.sqrt(1.0 - now_bar) * noise_pred) / jnp.sqrt(now_bar)
    denoised = jnp.sqrt(prev_bar) * clean_latent + jnp.sqrt(1.0 - prev_bar) * noise_pred
    return (fresh[None, None], next_rows[None], noise_pred, denoised)


def solution(mesh):
    placed = (
        P("section", "req", None, None),
        P("section", "req"),
        P("section", "req", None, None),
        P("section", "req", None, None),
        P("req", None, None),
        P("section", "req", None, None),
        P("section", "req", None, None),
        P("section", "req", None, None),
        P("section", "req", None, None),
        P(),
        P("req", "section"),
        P("req"),
        P("req"),
    )
    return jax.shard_map(
        per_device,
        mesh=mesh,
        in_specs=placed,
        out_specs=(
            P("section", "req", None, None),
            P("req", "section", None),
            P("req", "section"),
            P("req", "section"),
        ),
        check_vma=False,
    )
```

profile of v0, /device:TPU:1, one launch (start us, length us, event | category | flops | bytes accessed | tf_op | source)
XLA Modules:
  0.0 108.0 jit_solution(940619815888001387)
XLA Ops:
  0.6 2.1 %copy.48 = bf16[1,1,128,2304]{3,2,1,0:T(8,128)(2,1)} copy(bf16[1,1,128,2304]{3,2,1,0:T(8,128)(2,1)} %param.15) | data formatting | bytes 1179648
  2.7 1.0 convert_reduce_fusion.1
  3.7 1.1 %fusion.40 = f32[32]{0:T(128)S(1)} fusion(bf16[1,1,32,1152]{3,2,1,0:T(8,128)(2,1)} %param.13, f32[32]{0:T(128)S(1)} %broadcast_multiply_fusion.2), kind=kLoop, calls=%fused_computation.41 | loop fusion | flops 147424 | bytes 73984 | tf_op jit(solution)/shard_map/reduce_sum | solution.py:24
  5.0 1.5 %slice_reduce_fusion.2 = (f32[1152]{0:T(1024)S(1)}, f32[1152]{0:T(1024)S(1)}, f32[1152]{0:T(1024)S(1)}, f32[1152]{0:T(1024)S(1)}, f32[1152]{0:T(1024)}, /*index=5*/f32[1152]{0:T(1024)}) fusion(f32[1,1,6,1152]{3,1,2,0:T(1,128)} %param.16), kind=kLoop, calls=%fused_computation.80 | loop fusion | flops 2304 | bytes 55296 | tf_op jit(solution)/shard_map/slice | solution.py:117
  6.4 1.0 fusion.44
  7.4 15.7 %all_to_all.30 = bf16[16,8,1152]{2,1,0:T(8,128)(2,1)S(1)} all-to-all(bf16[16,8,1152]{2,1,0:T(8,128)(2,1)S(1)} %bitcast.125), channel_id=1, replica_groups=mesh['section'=2,'req'=16] {'req'}, dimensions={0} | all-to-all | bytes 589824 | tf_op jit(solution)/shard_map/all_to_all | solution.py:88
  23.1 3.0 %fusion.11 = bf16[16,8,864]{2,1,0:T(8,128)(2,1)} fusion(bf16[16,8,1152]{2,1,0:T(8,128)(2,1)S(1)} %all_to_all.30, bf16[1,1,1152,864]{2,3,1,0:T(8,128)(2,1)} %param.18), kind=kOutput, calls=%fused_computation.9 | convolution fusion | flops 254914560 | bytes 2506752 | tf_op jit(solution)/shard_map/nsd,dc->nsc/dot_general | solution.py:63
  26.1 4.9 %all-to-all-start.1 = ((bf16[16,8,864]{2,1,0:T(8,128)(2,1)}), bf16[16,8,864]{2,1,0:T(8,128)(2,1)S(1)}, u32[]{:S(2)}, u32[]{:S(2)}) async-start(bf16[16,8,864]{2,1,0:T(8,128)(2,1)} %fusion.11), calls=%async_computation.1 | async-start | bytes 458752 | tf_op jit(solution)/shard_map/all_to_all | solution.py:87
  31.7 6.6 %all-to-all-done.1 = bf16[16,8,864]{2,1,0:T(8,128)(2,1)S(1)} async-done(((bf16[16,8,864]{2,1,0:T(8,128)(2,1)}), bf16[16,8,864]{2,1,0:T(8,128)(2,1)S(1)}, u32[]{:S(2)}, u32[]{:S(2)}) %all-to-all-start.1) | async-done | bytes 221216 | tf_op jit(solution)/shard_map/all_to_all | solution.py:87
  38.3 0.3 reshape_reshape.4
  38.6 0.5 fusion.73
  39.2 0.8 reshape_reshape_squeeze.3
  40.6 0.7 copy-done.2
  41.2 0.7 constant_dynamic-update-slice_fusion.2
  41.9 1.1 %fusion.72 = (bf16[128,1152]{1,0:T(8,128)(2,1)S(1)}, bf16[128,1152]{1,0:T(8,128)(2,1)S(1)}) fusion(bf16[128,2304]{1,0:T(8,128)(2,1)} %constant_dynamic-update-slice_fusion.2), kind=kLoop, calls=%fused_computation.97 | loop fusion | bytes 1179648 | tf_op jit(solution)/shard_map/slice | solution.py:42
  43.0 0.2 copy.32
  43.2 1.1 %convolution_multiply_fusion = f32[16,32,128]{2,1,0:T(8,128)S(1)} fusion(bf16[128,16,72]{0,2,1:T(8,128)(2,1)S(1)} %bitcast.128, bf16[32,16,72]{2,1,0:T(8,128)(2,1)} %reshape_reshape_squeeze.3), kind=kOutput, calls=%fused_computation.10 | convolution fusion | flops 9502720 | bytes 630784 | tf_op jit(solution)/shard_map/qhd,khd->hqk/dot_general | solution.py:44
  44.3 0.2 fusion.74
  44.6 0.2 copy.30
  44.8 1.6 %fusion.15 = bf16[32,16,72]{2,0,1:T(8,128)(2,1)} fusion(bf16[128,16,72]{0,2,1:T(8,128)(2,1)S(1)} %bitcast.133, f32[16,32]{1,0:T(8,128)S(1)} %fusion.74, f32[16,32,128]{2,1,0:T(8,128)S(1)} %convolution_multiply_fusion), kind=kOutput, calls=%fused_computation.14 | convolution fusion | flops 9671295 | bytes 632832 | tf_op jit(solution)/shard_map/hqk,khd->qhd/dot_general | solution.py:53
  46.4 1.0 copy.34
  47.5 12.4 %all_to_all.31 = bf16[16,8,1152]{2,1,0:T(8,128)(2,1)S(1)} all-to-all(bf16[16,8,1152]{2,1,0:T(8,128)(2,1)S(1)} %bitcast.126), channel_id=1, replica_groups=mesh['section'=2,'req'=16] {'req'}, dimensions={0} | all-to-all | bytes 589824 | tf_op jit(solution)/shard_map/all_to_all | solution.py:88
  59.9 1.5 %convolution_convert_fusion.1 = bf16[16,8,288]{2,1,0:T(8,128)(2,1)S(1)} fusion(bf16[16,8,1152]{2,1,0:T(8,128)(2,1)S(1)} %all_to_all.31, bf16[1,1,1152,288]{2,3,1,0:T(8,128)(2,1)} %param.19), kind=kOutput, calls=%fused_computation.13 | convolution fusion | flops 84971520 | bytes 1032192 | tf_op jit(solution)/shard_map/nsd,dc->nsc/dot_general | solution.py:63
  61.4 11.9 %all_to_all.32 = bf16[16,8,288]{2,1,0:T(8,128)(2,1)S(1)} all-to-all(bf16[16,8,288]{2,1,0:T(8,128)(2,1)S(1)} %convolution_convert_fusion.1), channel_id=1, replica_groups=mesh['section'=2,'req'=16] {'req'}, dimensions={0} | all-to-all | bytes 147456 | tf_op jit(solution)/shard_map/all_to_all | solution.py:87
  73.8 0.2 multiply_reduce_fusion
  74.3 10.3 %all_to_all.33 = bf16[16,8,1152]{2,1,0:T(8,128)(2,1)S(1)} all-to-all(bf16[16,8,1152]{2,1,0:T(8,128)(2,1)S(1)} %bitcast.127), channel_id=1, replica_groups=mesh['section'=2,'req'=16] {'req'}, dimensions={0} | all-to-all | bytes 589824 | tf_op jit(solution)/shard_map/all_to_all | solution.py:88
  84.6 3.6 %fusion.5 = bf16[16,8,1152]{2,1,0:T(8,128)(2,1)} fusion(bf16[1,1,1152,1152]{3,2,1,0:T(8,128)(2,1)S(1)} %copy-done, bf16[16,8,1152]{2,1,0:T(8,128)(2,1)S(1)} %all_to_all.33, bf16[1,1,1152,1152]{3,2,1,0:T(8,128)(2,1)} %param.20), kind=kOutput, calls=%fused_computation.5 | convolution fusion | flops 680951808 | bytes 5898240 | tf_op jit(solution)/shard_map/nsf,fd->nsd/dot_general | solution.py:73
  88.2 3.5 %all-to-all-start.5 = ((bf16[16,8,1152]{2,1,0:T(8,128)(2,1)}), bf16[16,8,1152]{2,1,0:T(8,128)(2,1)S(1)}, u32[]{:S(2)}, u32[]{:S(2)}) async-start(bf16[16,8,1152]{2,1,0:T(8,128)(2,1)} %fusion.5), calls=%async_computation.5 | async-start | bytes 589824 | tf_op jit(solution)/shard_map/all_to_all | solution.py:87
  91.7 7.5 %all-to-all-done.5 = bf16[16,8,1152]{2,1,0:T(8,128)(2,1)S(1)} async-done(((bf16[16,8,1152]{2,1,0:T(8,128)(2,1)}), bf16[16,8,1152]{2,1,0:T(8,128)(2,1)S(1)}, u32[]{:S(2)}, u32[]{:S(2)}) %all-to-all-start.5) | async-done | bytes 294944 | tf_op jit(solution)/shard_map/all_to_all | solution.py:87
  99.4 5.2 %collective-permute-start = (bf16[16,1152]{1,0:T(8,128)(2,1)S(1)}, bf16[16,1152]{1,0:T(8,128)(2,1)S(1)}, u32[]{:S(2)}, u32[]{:S(2)}) collective-permute-start(bf16[16,1152]{1,0:T(8,128)(2,1)S(1)} %broadcast_select_fusion.1), channel_id=1, source_target_pairs={{0,16},{16,0},{1,17},{17,1},{2,18},{18,2},{3,19},{19,3},{4,20},{20... | collective-permute-start | bytes 110600 | tf_op jit(solution)/shard_map/ppermute | solution.py:18
  106.8 0.6 multiply_add_fusion
  107.4 0.6 select_bitcast_fusion
  (53 shorter events, 2.6 us)
Async XLA Ops:
  0.6 84.0 %copy-start = (bf16[1,1,1152,1152]{3,2,1,0:T(8,128)(2,1)S(1)}, bf16[1,1,1152,1152]{3,2,1,0:T(8,128)(2,1)}, u32[]{:S(2)}) copy-start(bf16[1,1,1152,1152]{3,2,1,0:T(8,128)(2,1)} %param.21) | copy-start | bytes 7962628
  26.1 12.2 %all-to-all-start.1 = ((bf16[16,8,864]{2,1,0:T(8,128)(2,1)}), bf16[16,8,864]{2,1,0:T(8,128)(2,1)S(1)}, u32[]{:S(2)}, u32[]{:S(2)}) async-start(bf16[16,8,864]{2,1,0:T(8,128)(2,1)} %fusion.11), calls=%async_computation.1 | async-start | bytes 458752 | tf_op jit(solution)/shard_map/all_to_all | solution.py:87
  40.6 0.7 copy-start.2
  44.8 28.9 %copy-start.1 = (bf16[1,1,32,1152]{3,2,1,0:T(8,128)(2,1)S(1)}, bf16[1,1,32,1152]{3,2,1,0:T(8,128)(2,1)}, u32[]{:S(2)}) copy-start(bf16[1,1,32,1152]{3,2,1,0:T(8,128)(2,1)} %param.13) | copy-start | bytes 221188
  44.8 29.4 %copy-start.3 = (f32[1152]{0:T(1024)S(1)}, f32[1152]{0:T(1024)}, u32[]{:S(2)}) copy-start(f32[1152]{0:T(1024)} %get-tuple-element.8) | copy-start | bytes 13828
  44.8 29.4 %copy-start.4 = (f32[1152]{0:T(1024)S(1)}, f32[1152]{0:T(1024)}, u32[]{:S(2)}) copy-start(f32[1152]{0:T(1024)} %get-tuple-element.9) | copy-start | bytes 13828
  84.6 20.0 %copy-start.5 = (f32[1,2,1152]{2,1,0:T(2,128)S(1)}, f32[1,2,1152]{2,1,0:T(2,128)}, u32[]{:S(2)}) copy-start(f32[1,2,1152]{2,1,0:T(2,128)} %param.17) | copy-start | bytes 27652
  84.6 21.9 %copy-start.8 = (bf16[1152,16]{0,1:T(8,128)(2,1)S(1)}, bf16[1152,16]{0,1:T(8,128)(2,1)}, u32[]{:S(2)}) copy-start(bf16[1152,16]{0,1:T(8,128)(2,1)} %param.22) | copy-start | bytes 110596
  84.6 22.2 %copy-start.7 = (f32[1,256]{1,0:T(1,128)S(1)}, f32[1,256]{1,0:T(1,128)}, u32[]{:S(2)}) copy-start(f32[1,256]{1,0:T(1,128)} %param.23) | copy-start | bytes 3076
  88.2 11.1 %all-to-all-start.5 = ((bf16[16,8,1152]{2,1,0:T(8,128)(2,1)}), bf16[16,8,1152]{2,1,0:T(8,128)(2,1)S(1)}, u32[]{:S(2)}, u32[]{:S(2)}) async-start(bf16[16,8,1152]{2,1,0:T(8,128)(2,1)} %fusion.5), calls=%async_computation.5 | async-start | bytes 589824 | tf_op jit(solution)/shard_map/all_to_all | solution.py:87
  99.4 6.8 %collective-permute-start = (bf16[16,1152]{1,0:T(8,128)(2,1)S(1)}, bf16[16,1152]{1,0:T(8,128)(2,1)S(1)}, u32[]{:S(2)}, u32[]{:S(2)}) collective-permute-start(bf16[16,1152]{1,0:T(8,128)(2,1)S(1)} %broadcast_select_fusion.1), channel_id=1, source_target_pairs={{0,16},{16,0},{1,17},{17,1},{2,18},{18,2},{3,19},{19,3},{4,20},{20... | collective-permute-start | bytes 110600 | tf_op jit(solution)/shard_map/ppermute | solution.py:18
  106.8 1.2 %copy-start.6 = (f32[1,256]{1,0:T(1,128)}, f32[1,256]{1,0:T(1,128)S(1)}, u32[]{:S(2)}) copy-start(f32[1,256]{1,0:T(1,128)S(1)} %reshape.272) | copy-start | bytes 3076
where the time goes:
time: 109 us; the launch traced here: 108 us
  blocking collectives  50.2 us (46%)
  waiting for transfers between devices  14.1 us (13%)
  starting transfers between devices  13.7 us (13%)
  matrix products  10.9 us (10%)
  local copies, waits for them, and re-layouts  9.11 us (8%)
  other arithmetic  6.87 us (6%)
  between operations  3.09 us (3%)
    all_to_all x3, blocking collectives, spread_regroup(): lax.all_to_all(outgoing, 'req', split_axis=0, concat_axis=0, tiled=True)  38.4 us
    all_to_all x2, waiting for transfers between devices, spread_regroup(): lax.all_to_all(block_fn(lax.all_to_all(outgoing, 'req', split_axis=0, con...  14.1 us
    all_to_all x1, blocking collectives, spread_regroup(): lax.all_to_all(block_fn(lax.all_to_all(outgoing, 'req', split_axis=0, con...  11.9 us
    all_to_all x2, starting transfers between devices, spread_regroup(): lax.all_to_all(block_fn(lax.all_to_all(outgoing, 'req', split_axis=0, con...  8.46 us
    ppermute x1, starting transfers between devices, from_partner(): lax.ppermute(x, axis, [(i, i ^ 1 << bit) for i in range(lax.axis_size(axi...  5.21 us
    dot_general x2, matrix products, block_product(): jnp.einsum('nsd,dc->nsc', incoming, weight, preferred_element_type=jnp.fl...  4.46 us
    dot_general x1, matrix products, unit_block(): jnp.einsum('nsf,fd->nsd', inner, w_down, preferred_element_type=jnp.float32)  3.57 us
    unnamed x20, local copies, waits for them, and re-layouts  2.77 us
  transfers between devices with their start and end apart: 3, of which 2 were waited for; matrix products, arithmetic and copies ran while one was open for 0% of the time, Pallas kernels for 0%

commit v1 on v0

v1 whole, which is shorter than its diff:
```python
from functools import partial

import jax
import jax.numpy as jnp
from jax import lax
from jax.experimental import pallas as pl
from jax.experimental.pallas import tpu as pltpu
from jax.sharding import PartitionSpec as P

HEADS = 16
UNIT_GROUPS = 4
LANE_ROWS = 16


NORM_EPS = 1e-06
BETA_LOW = 0.0001
BETA_HIGH = 0.02

BF16 = jnp.bfloat16
F32 = jnp.float32
VMEM = pl.BlockSpec(memory_space=pltpu.VMEM)
SMEM = pl.BlockSpec(memory_space=pltpu.SMEM)
PARAMS = pltpu.CompilerParams(vmem_limit_bytes=32 * 1024 * 1024)


def layer_norm(values):
    average = jnp.mean(values, axis=-1, keepdims=True)
    centred = values - average
    spread = jnp.mean(centred * centred, axis=-1, keepdims=True)
    return centred * lax.rsqrt(spread + NORM_EPS)


def alpha_bar(moment):
    return jnp.exp(
        -(BETA_LOW * (moment + 1.0) + (BETA_HIGH - BETA_LOW) * moment * (moment + 1.0) / 1998.0)
    )


def own_block():
    return lax.rem(lax.axis_index("req"), UNIT_GROUPS)


def other_block(block, k):
    return lax.bitwise_xor(block, jnp.int32(k))


def swap(x, k):
    return lax.ppermute(x, "req", [(i, i ^ k) for i in range(lax.axis_size("req"))])


def call(body, outs, *args, smem=0, scratch=()):
    return pl.pallas_call(
        body,
        out_shape=outs,
        in_specs=[SMEM] * smem + [VMEM] * (len(args) - smem),
        out_specs=jax.tree.map(lambda _: VMEM, outs),
        scratch_shapes=list(scratch),
        compiler_params=PARAMS,
    )(*args)


def norm_kernel(hidden, mods, normed):
    values = layer_norm(hidden[...].astype(F32))
    normed[...] = (values * (1.0 + mods[1:2, :]) + mods[0:1, :]).astype(BF16)


def pack_kernel(patch, hidden, mods, stale, *rest):
    outs, packed = rest[:UNIT_GROUPS], rest[UNIT_GROUPS]
    fresh, width = hidden.shape
    part = width // UNIT_GROUPS
    kept = (stale.shape[0] // fresh - 1) * fresh
    patches = stale.shape[0] // fresh
    start = patch[0, 0]
    high = mods[2:6, :].astype(BF16).astype(F32)
    low = mods[2:6, :] - high
    pad = jnp.zeros((4, part), F32)
    for i in range(1, patches):
        source = pl.multiple_of(lax.rem(start + i, patches) * fresh, fresh)
        rows = stale[pl.ds(source, fresh), :]
        for block in range(UNIT_GROUPS):
            at = block * part
            packed[block, (i - 1) * fresh : i * fresh, :] = rows[:, at : at + part]
            packed[block, kept + (i - 1) * fresh : kept + i * fresh, :] = rows[:, width + at : width + at + part]
    for block in range(UNIT_GROUPS):
        at = block * part
        packed[block, 2 * kept : 2 * kept + fresh, :] = hidden[:, at : at + part]
        for other in range(UNIT_GROUPS):
            there = other * part
            rows = jnp.concatenate([high[:, there : there + part], pad, low[:, there : there + part], pad], axis=0)
            base = 2 * kept + fresh + other * LANE_ROWS
            packed[block, base : base + LANE_ROWS, :] = rows.astype(BF16)
    here = own_block()
    for k in range(UNIT_GROUPS):
        outs[k][...] = packed[other_block(here, k)]


def attend_kernel(n0, n1, n2, n3, p0, p1, p2, p3, weight, a0, a1, a2, a3):
    fresh, width = n0.shape
    part = width // UNIT_GROUPS
    heads = HEADS // UNIT_GROUPS
    head_size = part // heads
    kept = (p0.shape[0] - fresh - UNIT_GROUPS * LANE_ROWS) // 2
    tokens = jnp.concatenate([n0[...], n1[...], n2[...], n3[...]], axis=0)
    joined = jnp.dot(tokens, weight[...], preferred_element_type=F32).astype(BF16)
    lane = lax.broadcasted_iota(jnp.int32, (fresh, part), 1)
    inside = [(lane >= h * head_size) & (lane < (h + 1) * head_size) for h in range(heads)]
    mixed = []
    fresh_rows = []
    for m, packed in enumerate((p0, p1, p2, p3)):
        rows = joined[m * fresh : (m + 1) * fresh]
        q, k, v = rows[:, :part], rows[:, part : 2 * part], rows[:, 2 * part :]
        keys = jnp.concatenate([packed[:kept, :], k], axis=0)
        values = jnp.concatenate([packed[kept : 2 * kept, :], v], axis=0)
        zero = jnp.zeros_like(q)
        spread = jnp.concatenate([jnp.where(inside[h], q, zero) for h in range(heads)], axis=0)
        scores = lax.dot_general(
            spread, keys, (((1,), (1,)), ((), ())), preferred_element_type=F32
        ) * head_size ** (-0.5)
        raised = jnp.exp(scores - jnp.max(scores, axis=-1, keepdims=True))
        probs = (raised / jnp.sum(raised, axis=-1, keepdims=True)).astype(BF16)
        out = jnp.dot(probs, values, preferred_element_type=F32)
        total = jnp.where(inside[0], out[:fresh], 0.0)
        for h in range(1, heads):
            total = jnp.where(inside[h], out[h * fresh : (h + 1) * fresh], total)
        mixed.append(total.astype(BF16))
        fresh_rows.append((k, v))
    for k, out in enumerate((a0, a1, a2, a3)):
        for m in range(UNIT_GROUPS):
            out[m * fresh : (m + 1) * fresh, :] = mixed[k ^ m]
        base = UNIT_GROUPS * fresh
        out[base : base + fresh, :] = fresh_rows[k][0]
        out[base + fresh : base + 2 * fresh, :] = fresh_rows[k][1]


def mod_rows(packed, block, row):
    fresh_base = packed.shape[0] - UNIT_GROUPS * LANE_ROWS
    base = pl.multiple_of(fresh_base + block * LANE_ROWS, LANE_ROWS)
    rows = packed[pl.ds(base, LANE_ROWS), :].astype(F32)
    return rows[row - 2 : row - 1] + rows[row + 6 : row + 7]


def project_kernel(a0, a1, a2, a3, p0, p1, p2, p3, weight, h1, sent, fresh_kv):
    part = weight.shape[1]
    width = weight.shape[0]
    fresh = (a0.shape[0]) // (UNIT_GROUPS + 2)
    count = UNIT_GROUPS * fresh
    residual_at = p0.shape[0] - UNIT_GROUPS * LANE_ROWS - fresh
    here = own_block()
    total = jnp.zeros((count, part), F32)
    for k, mixed in enumerate((a0, a1, a2, a3)):
        rows = pl.ds(pl.multiple_of(other_block(here, k) * part, 32), part)
        total += jnp.dot(mixed[:count, :], weight[rows, :], preferred_element_type=F32)
    projected = total.astype(BF16).astype(F32)
    for m, packed in enumerate((p0, p1, p2, p3)):
        residual = packed[residual_at : residual_at + fresh, :].astype(F32)
        gate = mod_rows(packed, here, 2)
        rows = slice(m * fresh, (m + 1) * fresh)
        value = residual + gate * projected[rows]
        h1[rows, :] = value
        sent[rows, :] = value.astype(BF16)
    for block in range(UNIT_GROUPS):
        for k, mixed in enumerate((a0, a1, a2, a3)):

            @pl.when(other_block(here, k) == block)
            def _():
                at = block * part
                fresh_kv[:, at : at + part] = mixed[count : count + fresh, :]
                fresh_kv[:, width + at : width + at + part] = mixed[count + fresh : count + 2 * fresh, :]


def mlp_kernel(h0, h1, h2, h3, p0, p1, p2, p3, w_up, w_down, o0, o1, o2, o3):
    count, part = h0.shape
    fresh = count // UNIT_GROUPS
    width = part * UNIT_GROUPS
    here = own_block()
    packs = (p0, p1, p2, p3)
    pieces = [h0[...]]
    for k, piece in enumerate((h1, h2, h3), start=1):
        value = piece[...].astype(F32)
        pieces.append(
            jnp.concatenate([value[(k ^ m) * fresh : (k ^ m) * fresh + fresh] for m in range(UNIT_GROUPS)], axis=0)
        )
    average = sum(jnp.sum(piece, axis=-1, keepdims=True) for piece in pieces) / width
    centred = [piece - average for piece in pieces]
    spread = sum(jnp.sum(piece * piece, axis=-1, keepdims=True) for piece in centred) / width
    scale = lax.rsqrt(spread + NORM_EPS)
    inner = jnp.zeros((count, w_up.shape[1]), F32)
    for k in range(UNIT_GROUPS):
        block = other_block(here, k)
        normed = centred[k] * scale
        middle = jnp.concatenate(
            [
                (
                    normed[m * fresh : (m + 1) * fresh] * (1.0 + mod_rows(packed, block, 4))
                    + mod_rows(packed, block, 3)
                ).astype(BF16)
                for m, packed in enumerate(packs)
            ],
            axis=0,
        )
        rows = pl.ds(pl.multiple_of(block * part, 32), part)
        inner += jnp.dot(middle, w_up[rows, :], preferred_element_type=F32)
    inner = jax.nn.gelu(inner, approximate=True).astype(BF16)
    partial_out = jnp.dot(inner, w_down[...], preferred_element_type=F32)
    for m, out in enumerate((o0, o1, o2, o3)):
        rows = slice(m * fresh, (m + 1) * fresh)
        gate = jnp.concatenate([mod_rows(packs[m], block, 5) for block in range(UNIT_GROUPS)], axis=1)
        own = pieces[0][rows]
        placed = jnp.concatenate(
            [jnp.where(here == block, own, 0.0) for block in range(UNIT_GROUPS)], axis=1
        )
        out[...] = (gate * partial_out[rows] + placed).astype(BF16)


def total_kernel(o0, o1, o2, o3, kept, leaving):
    half = kept.shape[0]
    section = lax.axis_index("section")
    for out, at in ((kept, section), (leaving, 1 - section)):
        rows = pl.ds(pl.multiple_of(at * half, half), half)
        out[...] = (
            (o0[rows, :].astype(F32) + o1[rows, :].astype(F32))
            + (o2[rows, :].astype(F32) + o3[rows, :].astype(F32))
        ).astype(BF16)


def final_kernel(time_index, time_gap, kept, arrived, mods, weight, noisy, next_rows, noise, denoised):
    first = lax.axis_index("section") == 0
    next_rows[...] = jnp.where(first, kept[...], arrived[...])
    rows = jnp.where(first, arrived[...], kept[...]).astype(F32)
    shifted = (layer_norm(rows) * (1.0 + mods[1:2, :]) + mods[0:1, :]).astype(BF16)
    repeated = jnp.dot(shifted, weight[...], preferred_element_type=F32)
    count, columns = repeated.shape
    channels = columns // count
    lane = lax.broadcasted_iota(jnp.int32, repeated.shape, 1)
    token = lax.broadcasted_iota(jnp.int32, repeated.shape, 0)
    mine = (lane >= token * channels) & (lane < (token + 1) * channels)
    value = jnp.sum(jnp.where(mine, repeated, 0.0), axis=0, keepdims=True)
    noise[...] = value
    now = jnp.full(value.shape, time_index[0], jnp.int32).astype(F32)
    before = jnp.full(value.shape, time_index[0] - time_gap[0], jnp.int32).astype(F32)
    now_bar, prev_bar = alpha_bar(now), alpha_bar(before)
    clean = (noisy[...] - jnp.sqrt(1.0 - now_bar) * value) / jnp.sqrt(now_bar)
    denoised[...] = jnp.sqrt(prev_bar) * clean + jnp.sqrt(1.0 - prev_bar) * value


def per_device(
    section_in,
    patch_index,
    stale_kv,
    modulation,
    final_mod,
    qkv_blocks,
    out_blocks,
    up_blocks,
    down_blocks,
    final_weight,
    noisy_latent,
    time_index,
    time_gap,
):
    shape = jax.ShapeDtypeStruct
    hidden, mods, stale = section_in[0, 0], modulation[0, 0], stale_kv[0, 0]
    fresh, width = hidden.shape
    part = width // UNIT_GROUPS
    half = fresh // 2
    count = UNIT_GROUPS * fresh
    others = range(1, UNIT_GROUPS)

    normed = call(norm_kernel, shape((fresh, width), BF16), hidden, mods)
    slots = [normed] + [swap(normed, k) for k in others]
    pack_rows = 2 * (stale.shape[0] - fresh) + fresh + UNIT_GROUPS * LANE_ROWS
    packs = call(
        pack_kernel,
        [shape((pack_rows, part), BF16)] * UNIT_GROUPS,
        patch_index,
        hidden,
        mods,
        stale,
        smem=1,
        scratch=[pltpu.VMEM((UNIT_GROUPS, pack_rows, part), BF16)],
    )
    packs = [packs[0]] + [swap(packs[k], k) for k in others]
    mixed = call(
        attend_kernel,
        [shape((count + 2 * fresh, part), BF16)] * UNIT_GROUPS,
        *slots,
        *packs,
        qkv_blocks[0, 0],
    )
    mixed = [mixed[0]] + [swap(mixed[k], k) for k in others]
    h1, sent, fresh_kv = call(
        project_kernel,
        [shape((count, part), F32), shape((count, part), BF16), shape((fresh, 2 * width), BF16)],
        *mixed,
        *packs,
        out_blocks[0, 0],
    )
    pieces = [h1] + [swap(sent, k) for k in others]
    parts = call(
        mlp_kernel,
        [shape((fresh, width), BF16)] * UNIT_GROUPS,
        *pieces,
        *packs,
        up_blocks[0, 0],
        down_blocks[0, 0],
    )
    parts = [parts[0]] + [swap(parts[k], k) for k in others]
    kept, leaving = call(total_kernel, [shape((half, width), BF16)] * 2, *parts)
    arrived = lax.ppermute(leaving, "section", [(0, 1), (1, 0)])
    next_rows, noise, denoised = call(
        final_kernel,
        [shape((half, width), BF16), shape(noisy_latent.shape, F32), shape(noisy_latent.shape, F32)],
        time_index,
        time_gap,
        kept,
        arrived,
        final_mod[0],
        jnp.tile(final_weight, (1, half)),
        noisy_latent,
        smem=2,
    )
    return (fresh_kv[None, None], next_rows[None], noise, denoised)


def solution(mesh):
    placed = (
        P("section", "req", None, None),
        P("section", "req"),
        P("section", "req", None, None),
        P("section", "req", None, None),
        P("req", None, None),
        P("section", "req", None, None),
        P("section", "req", None, None),
        P("section", "req", None, None),
        P("section", "req", None, None),
        P(),
        P("req", "section"),
        P("req"),
        P("req"),
    )
    return jax.shard_map(
        per_device,
        mesh=mesh,
        in_specs=placed,
        out_specs=(
            P("section", "req", None, None),
            P("req", "section", None),
            P("req", "section"),
            P("req", "section"),
        ),
        check_vma=False,
    )
```

time: 109 us -> 68.5 us (0.63)
  blocking collectives: 50.2 us -> 0 us
  matrix products: 10.9 us -> 0 us
  Pallas kernels: 0 us -> 9.18 us
  starting transfers between devices: 13.7 us -> 22.6 us
  local copies, waits for them, and re-layouts: 9.11 us -> 16.5 us
  other arithmetic: 6.87 us -> 0 us
  waiting for transfers between devices: 14.1 us -> 16.9 us
    all_to_all x4 -> x0, blocking collectives: 50.2 us -> none  [the longest x3 38.4 us: spread_regroup(): lax.all_to_all(outgoing, 'req', split_axis=0, concat_axis=0, tiled=True)]
    ppermute x1 -> x16, starting transfers between devices: 5.21 us -> 22.6 us  [the longest x15 16.1 us: swap(): lax.ppermute(x, 'req', [(i, i ^ k) for i in range(lax.axis_size('req'))])]
    ppermute x1 -> x16, waiting for transfers between devices: 0.01 us -> 16.9 us  [the longest x15 16.9 us: swap(): lax.ppermute(x, 'req', [(i, i ^ k) for i in range(lax.axis_size('req'))])]
    all_to_all x2 -> x0, waiting for transfers between devices: 14.1 us -> none  [spread_regroup(): lax.all_to_all(block_fn(lax.all_to_all(outgoing, 'req', split_axis=0, con...]
    unnamed x20 -> x37, local copies, waits for them, and re-layouts: 2.77 us -> 16.2 us
    dot_general x6 -> x0, matrix products: 10.9 us -> none  [the longest x2 4.46 us: block_product(): jnp.einsum('nsd,dc->nsc', incoming, weight, preferred_element_type=jnp.fl...]
    pallas_call x0 -> x7, Pallas kernels: none -> 9.18 us  [call(): pl.pallas_call(body, out_shape=outs, in_specs=[SMEM] * smem + [VMEM] * (l...]
    all_to_all x2 -> x0, starting transfers between devices: 8.46 us -> none  [spread_regroup(): lax.all_to_all(block_fn(lax.all_to_all(outgoing, 'req', split_axis=0, con...]
  transfers between devices with their start and end apart: 3 -> 16, of which waited for: 2 -> 10; matrix products, arithmetic and copies ran while one was open for 0% -> 7% of each run, Pallas kernels for 0% -> 0%
where the time goes in v1:
time: 68.5 us; the launch traced here: 68 us
  starting transfers between devices  22.6 us (33%)
  waiting for transfers between devices  16.9 us (25%)
  local copies, waits for them, and re-layouts  16.5 us (24%)
  Pallas kernels  9.18 us (13%)
  between operations  2.73 us (4%)
    ppermute x15, waiting for transfers between devices, swap(): lax.ppermute(x, 'req', [(i, i ^ k) for i in range(lax.axis_size('req'))])  16.9 us
    unnamed x37, local copies, waits for them, and re-layouts  16.2 us
    ppermute x15, starting transfers between devices, swap(): lax.ppermute(x, 'req', [(i, i ^ k) for i in range(lax.axis_size('req'))])  16.1 us
    pallas_call x7, Pallas kernels, call(): pl.pallas_call(body, out_shape=outs, in_specs=[SMEM] * smem + [VMEM] * (l...  9.18 us
    ppermute x1, starting transfers between devices, per_device(): arrived = lax.ppermute(leaving, 'section', [(0, 1), (1, 0)])  6.5 us
  transfers between devices with their start and end apart: 16, of which 10 were waited for; matrix products, arithmetic and copies ran while one was open for 7% of the time, Pallas kernels for 0%

profile of v1, /device:TPU:1, one launch (start us, length us, event | category | flops | bytes accessed | tf_op | source)
XLA Modules:
  0.0 68.0 jit_solution(11432211011219568483)
XLA Ops:
  2.0 1.1 %copy-done.10 = bf16[1,1,128,2304]{3,2,1,0:T(8,128)(2,1)S(1)} copy-done((bf16[1,1,128,2304]{3,2,1,0:T(8,128)(2,1)S(1)}, bf16[1,1,128,2304]{3,2,1,0:T(8,128)(2,1)}, u32[]{:S(2)}) %copy-start.10) | copy-done | bytes 589848
  3.1 0.9 %copy-done.11 = bf16[1,1,32,1152]{3,2,1,0:T(8,128)(2,1)S(1)} copy-done((bf16[1,1,32,1152]{3,2,1,0:T(8,128)(2,1)S(1)}, bf16[1,1,32,1152]{3,2,1,0:T(8,128)(2,1)}, u32[]{:S(2)}) %copy-start.11) | copy-done | bytes 73752
  4.0 1.1 %shard_map.157 = (bf16[288,288]{1,0:T(8,128)(2,1)S(1)}, bf16[288,288]{1,0:T(8,128)(2,1)}, bf16[288,288]{1,0:T(8,128)(2,1)}, bf16[288,288]{1,0:T(8,128)(2,1)S(1)}) custom-call(s32[1,1]{1,0:T(1,128)S(6)} %copy.26.patch, bf16[32,1152]{1,0:T(8,128)(2,1)S(1)} %bitcast.20, f32[6,1152]{1,0:T(8,128)S(1)} %bitcast.18, bf16[128,2304]{1,0:T(8,128)(2,1)S(1)} %bitcast.17), custom_call_target="tpu_custom_call" | custom-call | tf_op jit(solution)/shard_map/pallas_call | solution.py:52
  5.1 2.0 %collective-permute-start.3 = (bf16[288,288]{1,0:T(8,128)(2,1)}, bf16[288,288]{1,0:T(8,128)(2,1)S(1)}, u32[]{:S(2)}, u32[]{:S(2)}) collective-permute-start(bf16[288,288]{1,0:T(8,128)(2,1)} %get-tuple-element.25), channel_id=1, source_target_pairs={{0,1},{1,0},{2,3},{3,2},{4,5},{5,4},{6,7},{7,6},{8,9},{9,8},{10,11... | collective-permute-start | bytes 497672 | tf_op jit(solution)/shard_map/ppermute | solution.py:48
  7.2 1.3 %collective-permute-start.4 = (bf16[288,288]{1,0:T(8,128)(2,1)}, bf16[288,288]{1,0:T(8,128)(2,1)S(1)}, u32[]{:S(2)}, u32[]{:S(2)}) collective-permute-start(bf16[288,288]{1,0:T(8,128)(2,1)} %get-tuple-element.26), channel_id=1, source_target_pairs={{0,2},{1,3},{2,0},{3,1},{4,6},{5,7},{6,4},{7,5},{8,10},{9,11},{10,... | collective-permute-start | bytes 497672 | tf_op jit(solution)/shard_map/ppermute | solution.py:48
  8.6 1.5 %collective-permute-start = (bf16[32,1152]{1,0:T(8,128)(2,1)S(1)}, bf16[32,1152]{1,0:T(8,128)(2,1)S(1)}, u32[]{:S(2)}, u32[]{:S(2)}) collective-permute-start(bf16[32,1152]{1,0:T(8,128)(2,1)S(1)} %shard_map.156.n0), channel_id=1, source_target_pairs={{0,1},{1,0},{2,3},{3,2},{4,5},{5,4},{6,7},{7,6},{8,9},{9,8},{10,11... | collective-permute-start | bytes 221192 | tf_op jit(solution)/shard_map/ppermute | solution.py:48
  10.1 1.3 %collective-permute-start.1 = (bf16[32,1152]{1,0:T(8,128)(2,1)S(1)}, bf16[32,1152]{1,0:T(8,128)(2,1)S(1)}, u32[]{:S(2)}, u32[]{:S(2)}) collective-permute-start(bf16[32,1152]{1,0:T(8,128)(2,1)S(1)} %shard_map.156.n0), channel_id=1, source_target_pairs={{0,2},{1,3},{2,0},{3,1},{4,6},{5,7},{6,4},{7,5},{8,10},{9,11},{10,... | collective-permute-start | bytes 221192 | tf_op jit(solution)/shard_map/ppermute | solution.py:48
  11.3 7.6 %collective-permute-done.n1 = bf16[32,1152]{1,0:T(8,128)(2,1)S(1)} collective-permute-done((bf16[32,1152]{1,0:T(8,128)(2,1)S(1)}, bf16[32,1152]{1,0:T(8,128)(2,1)S(1)}, u32[]{:S(2)}, u32[]{:S(2)}) %collective-permute-start) | collective-permute-done | bytes 73760 | tf_op jit(solution)/shard_map/ppermute | solution.py:48
  18.9 2.1 %collective-permute-start.2 = (bf16[32,1152]{1,0:T(8,128)(2,1)S(1)}, bf16[32,1152]{1,0:T(8,128)(2,1)S(1)}, u32[]{:S(2)}, u32[]{:S(2)}) collective-permute-start(bf16[32,1152]{1,0:T(8,128)(2,1)S(1)} %shard_map.156.n0), channel_id=1, source_target_pairs={{0,3},{1,2},{2,1},{3,0},{4,7},{5,6},{6,5},{7,4},{8,11},{9,10},{10,... | collective-permute-start | bytes 221192 | tf_op jit(solution)/shard_map/ppermute | solution.py:48
  21.0 2.9 %copy.20 = bf16[1,1,1152,864]{3,2,1,0:T(8,128)(2,1)S(1)} copy(bf16[1,1,1152,864]{2,3,1,0:T(8,128)(2,1)} %param.18) | data formatting | bytes 3981312 | tf_op args[5]
  23.9 2.9 %shard_map.158 = (bf16[192,288]{1,0:T(8,128)(2,1)S(1)}, bf16[192,288]{1,0:T(8,128)(2,1)}, bf16[192,288]{1,0:T(8,128)(2,1)}, bf16[192,288]{1,0:T(8,128)(2,1)}) custom-call(bf16[32,1152]{1,0:T(8,128)(2,1)S(1)} %shard_map.156.n0, bf16[32,1152]{1,0:T(8,128)(2,1)S(1)} %collective-permute-done.n1, bf16[32,1152]{1,0:T(8,128)(2,1)S(1)} %collective-permute-done.1.n2, ...), custom_call_target="tpu_custom_call" | custom-call | tf_op jit(solution)/shard_map/pallas_call | solution.py:52
  29.8 1.2 %collective-permute-start.7 = (bf16[192,288]{1,0:T(8,128)(2,1)}, bf16[192,288]{1,0:T(8,128)(2,1)}, u32[]{:S(2)}, u32[]{:S(2)}) collective-permute-start(bf16[192,288]{1,0:T(8,128)(2,1)} %get-tuple-element.30), channel_id=1, source_target_pairs={{0,2},{1,3},{2,0},{3,1},{4,6},{5,7},{6,4},{7,5},{8,10},{9,11},{10,... | collective-permute-start | bytes 331784 | tf_op jit(solution)/shard_map/ppermute | solution.py:48
  31.0 1.2 %collective-permute-start.8 = (bf16[192,288]{1,0:T(8,128)(2,1)}, bf16[192,288]{1,0:T(8,128)(2,1)}, u32[]{:S(2)}, u32[]{:S(2)}) collective-permute-start(bf16[192,288]{1,0:T(8,128)(2,1)} %get-tuple-element.31), channel_id=1, source_target_pairs={{0,3},{1,2},{2,1},{3,0},{4,7},{5,6},{6,5},{7,4},{8,11},{9,10},{10,... | collective-permute-start | bytes 331784 | tf_op jit(solution)/shard_map/ppermute | solution.py:48
  32.2 1.5 %copy.21 = bf16[1,1,1152,288]{3,2,1,0:T(8,128)(2,1)S(1)} copy(bf16[1,1,1152,288]{2,3,1,0:T(8,128)(2,1)} %param.19) | data formatting | bytes 1327104 | tf_op args[6]
  34.3 2.7 %collective-permute-done.8.a3 = bf16[192,288]{1,0:T(8,128)(2,1)} collective-permute-done((bf16[192,288]{1,0:T(8,128)(2,1)}, bf16[192,288]{1,0:T(8,128)(2,1)}, u32[]{:S(2)}, u32[]{:S(2)}) %collective-permute-start.8) | collective-permute-done | bytes 110624 | tf_op jit(solution)/shard_map/ppermute | solution.py:48
  37.1 0.9 %copy-done.3 = bf16[288,288]{1,0:T(8,128)(2,1)S(1)} copy-done((bf16[288,288]{1,0:T(8,128)(2,1)S(1)}, bf16[288,288]{1,0:T(8,128)(2,1)}, u32[]{:S(2)}) %copy-start.3) | copy-done | bytes 165912
  38.0 0.9 %copy-done.5 = bf16[288,288]{1,0:T(8,128)(2,1)S(1)} copy-done((bf16[288,288]{1,0:T(8,128)(2,1)S(1)}, bf16[288,288]{1,0:T(8,128)(2,1)}, u32[]{:S(2)}) %copy-start.5) | copy-done | bytes 165912
  39.0 0.9 %copy-done.7 = bf16[288,288]{1,0:T(8,128)(2,1)S(1)} copy-done((bf16[288,288]{1,0:T(8,128)(2,1)S(1)}, bf16[288,288]{1,0:T(8,128)(2,1)}, u32[]{:S(2)}) %copy-start.7) | copy-done | bytes 165912
  39.9 0.9 %copy-done.9 = bf16[288,288]{1,0:T(8,128)(2,1)S(1)} copy-done((bf16[288,288]{1,0:T(8,128)(2,1)S(1)}, bf16[288,288]{1,0:T(8,128)(2,1)}, u32[]{:S(2)}) %copy-start.9) | copy-done | bytes 165912
  40.8 0.9 %copy-done.13 = bf16[192,288]{1,0:T(8,128)(2,1)S(1)} copy-done((bf16[192,288]{1,0:T(8,128)(2,1)S(1)}, bf16[192,288]{1,0:T(8,128)(2,1)}, u32[]{:S(2)}) %copy-start.13) | copy-done | bytes 110616
  41.7 2.4 %shard_map.159 = (f32[128,288]{1,0:T(8,128)S(1)}, bf16[128,288]{1,0:T(8,128)(2,1)S(1)}, bf16[32,2304]{1,0:T(8,128)(2,1)}) custom-call(bf16[192,288]{1,0:T(8,128)(2,1)S(1)} %copy-done.13, bf16[192,288]{1,0:T(8,128)(2,1)} %collective-permute-done.6.a1, bf16[192,288]{1,0:T(8,128)(2,1)} %collective-permute-done.7.a2, ...), custom_call_target="tpu_custom_call" | custom-call | tf_op jit(solution)/shard_map/pallas_call | solution.py:52
  44.5 1.1 %collective-permute-start.11 = (bf16[128,288]{1,0:T(8,128)(2,1)S(1)}, bf16[128,288]{1,0:T(8,128)(2,1)S(1)}, u32[]{:S(2)}, u32[]{:S(2)}) collective-permute-start(bf16[128,288]{1,0:T(8,128)(2,1)S(1)} %get-tuple-element.34), channel_id=1, source_target_pairs={{0,3},{1,2},{2,1},{3,0},{4,7},{5,6},{6,5},{7,4},{8,11},{9,10},{10,... | collective-permute-start | bytes 221192 | tf_op jit(solution)/shard_map/ppermute | solution.py:48
  45.5 1.3 %collective-permute-start.9 = (bf16[128,288]{1,0:T(8,128)(2,1)S(1)}, bf16[128,288]{1,0:T(8,128)(2,1)S(1)}, u32[]{:S(2)}, u32[]{:S(2)}) collective-permute-start(bf16[128,288]{1,0:T(8,128)(2,1)S(1)} %get-tuple-element.34), channel_id=1, source_target_pairs={{0,1},{1,0},{2,3},{3,2},{4,5},{5,4},{6,7},{7,6},{8,9},{9,8},{10,11... | collective-permute-start | bytes 221192 | tf_op jit(solution)/shard_map/ppermute | solution.py:48
  47.6 1.2 %collective-permute-done.11.h3 = bf16[128,288]{1,0:T(8,128)(2,1)S(1)} collective-permute-done((bf16[128,288]{1,0:T(8,128)(2,1)S(1)}, bf16[128,288]{1,0:T(8,128)(2,1)S(1)}, u32[]{:S(2)}, u32[]{:S(2)}) %collective-permute-start.11) | collective-permute-done | bytes 73760 | tf_op jit(solution)/shard_map/ppermute | solution.py:48
  48.8 1.0 %collective-permute-done.9.h1 = bf16[128,288]{1,0:T(8,128)(2,1)S(1)} collective-permute-done((bf16[128,288]{1,0:T(8,128)(2,1)S(1)}, bf16[128,288]{1,0:T(8,128)(2,1)S(1)}, u32[]{:S(2)}, u32[]{:S(2)}) %collective-permute-start.9) | collective-permute-done | bytes 73760 | tf_op jit(solution)/shard_map/ppermute | solution.py:48
  49.9 1.7 %copy-done.1 = bf16[1,1,1152,1152]{3,2,1,0:T(8,128)(2,1)S(1)} copy-done((bf16[1,1,1152,1152]{3,2,1,0:T(8,128)(2,1)S(1)}, bf16[1,1,1152,1152]{3,2,1,0:T(8,128)(2,1)}, u32[]{:S(2)}) %copy-start.1) | copy-done | bytes 2654232
  51.6 1.6 %shard_map.160 = (bf16[32,1152]{1,0:T(8,128)(2,1)S(1)}, bf16[32,1152]{1,0:T(8,128)(2,1)S(1)}, bf16[32,1152]{1,0:T(8,128)(2,1)S(1)}, bf16[32,1152]{1,0:T(8,128)(2,1)S(1)}) custom-call(f32[128,288]{1,0:T(8,128)S(1)} %get-tuple-element.33.h0, bf16[128,288]{1,0:T(8,128)(2,1)S(1)} %collective-permute-done.9.h1, bf16[128,288]{1,0:T(8,128)(2,1)S(1)} %collective-permute-done.10.h2, ...), custom_call_target="tpu_custom_call" | custom-call | tf_op jit(solution)/shard_map/pallas_call | solution.py:52
  53.7 1.0 %collective-permute-start.13 = (bf16[32,1152]{1,0:T(8,128)(2,1)S(1)}, bf16[32,1152]{1,0:T(8,128)(2,1)S(1)}, u32[]{:S(2)}, u32[]{:S(2)}) collective-permute-start(bf16[32,1152]{1,0:T(8,128)(2,1)S(1)} %get-tuple-element.37), channel_id=1, source_target_pairs={{0,2},{1,3},{2,0},{3,1},{4,6},{5,7},{6,4},{7,5},{8,10},{9,11},{10,... | collective-permute-start | bytes 221192 | tf_op jit(solution)/shard_map/ppermute | solution.py:48
  54.7 1.2 %collective-permute-start.14 = (bf16[32,1152]{1,0:T(8,128)(2,1)S(1)}, bf16[32,1152]{1,0:T(8,128)(2,1)S(1)}, u32[]{:S(2)}, u32[]{:S(2)}) collective-permute-start(bf16[32,1152]{1,0:T(8,128)(2,1)S(1)} %get-tuple-element.38), channel_id=1, source_target_pairs={{0,3},{1,2},{2,1},{3,0},{4,7},{5,6},{6,5},{7,4},{8,11},{9,10},{10,... | collective-permute-start | bytes 221192 | tf_op jit(solution)/shard_map/ppermute | solution.py:48
  56.9 1.9 %collective-permute-done.14.o3 = bf16[32,1152]{1,0:T(8,128)(2,1)S(1)} collective-permute-done((bf16[32,1152]{1,0:T(8,128)(2,1)S(1)}, bf16[32,1152]{1,0:T(8,128)(2,1)S(1)}, u32[]{:S(2)}, u32[]{:S(2)}) %collective-permute-start.14) | collective-permute-done | bytes 73760 | tf_op jit(solution)/shard_map/ppermute | solution.py:48
  58.9 6.5 %collective-permute-start.15 = (bf16[16,1152]{1,0:T(8,128)(2,1)S(1)}, bf16[16,1152]{1,0:T(8,128)(2,1)S(1)}, u32[]{:S(2)}, u32[]{:S(2)}) collective-permute-start(bf16[16,1152]{1,0:T(8,128)(2,1)S(1)} %get-tuple-element.40), channel_id=1, source_target_pairs={{0,16},{16,0},{1,17},{17,1},{2,18},{18,2},{3,19},{19,3},{4,20},{20... | collective-permute-start | bytes 110600 | tf_op jit(solution)/shard_map/ppermute | solution.py:309
  67.0 0.9 %shard_map.162 = (bf16[16,1152]{1,0:T(8,128)(2,1)}, f32[1,256]{1,0:T(1,128)}, f32[1,256]{1,0:T(1,128)}) custom-call(s32[1]{0:T(128)S(6)} %copy.27.time_index, s32[1]{0:T(128)S(6)} %copy.28.time_gap, bf16[16,1152]{1,0:T(8,128)(2,1)S(1)} %get-tuple-element.39.kept, bf16[16,1152]{1,0:T(8,128)(2,1)S(1)} %collective-permute-done.15.arrived, ...), custom_call_target="tpu_custom_call" | custom-call | tf_op jit(solution)/shard_map/pallas_call | solution.py:52
  (46 shorter events, 7.6 us)
Async XLA Ops:
  2.0 1.1 %copy-start.10 = (bf16[1,1,128,2304]{3,2,1,0:T(8,128)(2,1)S(1)}, bf16[1,1,128,2304]{3,2,1,0:T(8,128)(2,1)}, u32[]{:S(2)}) copy-start(bf16[1,1,128,2304]{3,2,1,0:T(8,128)(2,1)} %param.15) | copy-start | bytes 1769476
  3.1 0.9 %copy-start.11 = (bf16[1,1,32,1152]{3,2,1,0:T(8,128)(2,1)S(1)}, bf16[1,1,32,1152]{3,2,1,0:T(8,128)(2,1)}, u32[]{:S(2)}) copy-start(bf16[1,1,32,1152]{3,2,1,0:T(8,128)(2,1)} %param.13) | copy-start | bytes 221188
  5.1 18.8 %copy-start.2 = (bf16[288,288]{1,0:T(8,128)(2,1)}, bf16[288,288]{1,0:T(8,128)(2,1)S(1)}, u32[]{:S(2)}) copy-start(bf16[288,288]{1,0:T(8,128)(2,1)S(1)} %get-tuple-element.24.p0) | copy-start | bytes 497668
  5.1 18.8 %collective-permute-start.3 = (bf16[288,288]{1,0:T(8,128)(2,1)}, bf16[288,288]{1,0:T(8,128)(2,1)S(1)}, u32[]{:S(2)}, u32[]{:S(2)}) collective-permute-start(bf16[288,288]{1,0:T(8,128)(2,1)} %get-tuple-element.25), channel_id=1, source_target_pairs={{0,1},{1,0},{2,3},{3,2},{4,5},{5,4},{6,7},{7,6},{8,9},{9,8},{10,11... | collective-permute-start | bytes 497672 | tf_op jit(solution)/shard_map/ppermute | solution.py:48
  7.2 16.7 %collective-permute-start.4 = (bf16[288,288]{1,0:T(8,128)(2,1)}, bf16[288,288]{1,0:T(8,128)(2,1)S(1)}, u32[]{:S(2)}, u32[]{:S(2)}) collective-permute-start(bf16[288,288]{1,0:T(8,128)(2,1)} %get-tuple-element.26), channel_id=1, source_target_pairs={{0,2},{1,3},{2,0},{3,1},{4,6},{5,7},{6,4},{7,5},{8,10},{9,11},{10,... | collective-permute-start | bytes 497672 | tf_op jit(solution)/shard_map/ppermute | solution.py:48
  8.4 15.5 %collective-permute-start.5 = (bf16[288,288]{1,0:T(8,128)(2,1)S(1)}, bf16[288,288]{1,0:T(8,128)(2,1)S(1)}, u32[]{:S(2)}, u32[]{:S(2)}) collective-permute-start(bf16[288,288]{1,0:T(8,128)(2,1)S(1)} %get-tuple-element.27), channel_id=1, source_target_pairs={{0,3},{1,2},{2,1},{3,0},{4,7},{5,6},{6,5},{7,4},{8,11},{9,10},{10,... | collective-permute-start | bytes 497672 | tf_op jit(solution)/shard_map/ppermute | solution.py:48
  8.6 10.3 %collective-permute-start = (bf16[32,1152]{1,0:T(8,128)(2,1)S(1)}, bf16[32,1152]{1,0:T(8,128)(2,1)S(1)}, u32[]{:S(2)}, u32[]{:S(2)}) collective-permute-start(bf16[32,1152]{1,0:T(8,128)(2,1)S(1)} %shard_map.156.n0), channel_id=1, source_target_pairs={{0,1},{1,0},{2,3},{3,2},{4,5},{5,4},{6,7},{7,6},{8,9},{9,8},{10,11... | collective-permute-start | bytes 221192 | tf_op jit(solution)/shard_map/ppermute | solution.py:48
  10.1 13.8 %collective-permute-start.1 = (bf16[32,1152]{1,0:T(8,128)(2,1)S(1)}, bf16[32,1152]{1,0:T(8,128)(2,1)S(1)}, u32[]{:S(2)}, u32[]{:S(2)}) collective-permute-start(bf16[32,1152]{1,0:T(8,128)(2,1)S(1)} %shard_map.156.n0), channel_id=1, source_target_pairs={{0,2},{1,3},{2,0},{3,1},{4,6},{5,7},{6,4},{7,5},{8,10},{9,11},{10,... | collective-permute-start | bytes 221192 | tf_op jit(solution)/shard_map/ppermute | solution.py:48
  18.9 5.0 %collective-permute-start.2 = (bf16[32,1152]{1,0:T(8,128)(2,1)S(1)}, bf16[32,1152]{1,0:T(8,128)(2,1)S(1)}, u32[]{:S(2)}, u32[]{:S(2)}) collective-permute-start(bf16[32,1152]{1,0:T(8,128)(2,1)S(1)} %shard_map.156.n0), channel_id=1, source_target_pairs={{0,3},{1,2},{2,1},{3,0},{4,7},{5,6},{6,5},{7,4},{8,11},{9,10},{10,... | collective-permute-start | bytes 221192 | tf_op jit(solution)/shard_map/ppermute | solution.py:48
  26.8 0.7 copy-start.4
  27.5 0.7 %copy-start.6 = (bf16[288,288]{1,0:T(8,128)(2,1)}, bf16[288,288]{1,0:T(8,128)(2,1)S(1)}, u32[]{:S(2)}) copy-start(bf16[288,288]{1,0:T(8,128)(2,1)S(1)} %collective-permute-done.4.p2) | copy-start | bytes 497668
  28.2 0.7 %copy-start.8 = (bf16[288,288]{1,0:T(8,128)(2,1)}, bf16[288,288]{1,0:T(8,128)(2,1)S(1)}, u32[]{:S(2)}) copy-start(bf16[288,288]{1,0:T(8,128)(2,1)S(1)} %collective-permute-done.5.p3) | copy-start | bytes 497668
  29.5 20.3 %copy-start = (bf16[1,1,1152,1152]{3,2,1,0:T(8,128)(2,1)S(1)}, bf16[1,1,1152,1152]{3,2,1,0:T(8,128)(2,1)}, u32[]{:S(2)}) copy-start(bf16[1,1,1152,1152]{3,2,1,0:T(8,128)(2,1)} %param.20) | copy-start | bytes 7962628
  29.5 4.3 %collective-permute-start.6 = (bf16[192,288]{1,0:T(8,128)(2,1)}, bf16[192,288]{1,0:T(8,128)(2,1)}, u32[]{:S(2)}, u32[]{:S(2)}) collective-permute-start(bf16[192,288]{1,0:T(8,128)(2,1)} %get-tuple-element.29), channel_id=1, source_target_pairs={{0,1},{1,0},{2,3},{3,2},{4,5},{5,4},{6,7},{7,6},{8,9},{9,8},{10,11... | collective-permute-start | bytes 331784 | tf_op jit(solution)/shard_map/ppermute | solution.py:48
  29.8 4.6 %collective-permute-start.7 = (bf16[192,288]{1,0:T(8,128)(2,1)}, bf16[192,288]{1,0:T(8,128)(2,1)}, u32[]{:S(2)}, u32[]{:S(2)}) collective-permute-start(bf16[192,288]{1,0:T(8,128)(2,1)} %get-tuple-element.30), channel_id=1, source_target_pairs={{0,2},{1,3},{2,0},{3,1},{4,6},{5,7},{6,4},{7,5},{8,10},{9,11},{10,... | collective-permute-start | bytes 331784 | tf_op jit(solution)/shard_map/ppermute | solution.py:48
  31.0 6.1 %collective-permute-start.8 = (bf16[192,288]{1,0:T(8,128)(2,1)}, bf16[192,288]{1,0:T(8,128)(2,1)}, u32[]{:S(2)}, u32[]{:S(2)}) collective-permute-start(bf16[192,288]{1,0:T(8,128)(2,1)} %get-tuple-element.31), channel_id=1, source_target_pairs={{0,3},{1,2},{2,1},{3,0},{4,7},{5,6},{6,5},{7,4},{8,11},{9,10},{10,... | collective-permute-start | bytes 331784 | tf_op jit(solution)/shard_map/ppermute | solution.py:48
  37.1 0.9 %copy-start.3 = (bf16[288,288]{1,0:T(8,128)(2,1)S(1)}, bf16[288,288]{1,0:T(8,128)(2,1)}, u32[]{:S(2)}) copy-start(bf16[288,288]{1,0:T(8,128)(2,1)} %copy-done.2) | copy-start | bytes 497668
  38.0 0.9 %copy-start.5 = (bf16[288,288]{1,0:T(8,128)(2,1)S(1)}, bf16[288,288]{1,0:T(8,128)(2,1)}, u32[]{:S(2)}) copy-start(bf16[288,288]{1,0:T(8,128)(2,1)} %copy-done.4) | copy-start | bytes 497668
  39.0 0.9 %copy-start.7 = (bf16[288,288]{1,0:T(8,128)(2,1)S(1)}, bf16[288,288]{1,0:T(8,128)(2,1)}, u32[]{:S(2)}) copy-start(bf16[288,288]{1,0:T(8,128)(2,1)} %copy-done.6) | copy-start | bytes 497668
  39.9 0.9 %copy-start.9 = (bf16[288,288]{1,0:T(8,128)(2,1)S(1)}, bf16[288,288]{1,0:T(8,128)(2,1)}, u32[]{:S(2)}) copy-start(bf16[288,288]{1,0:T(8,128)(2,1)} %copy-done.8) | copy-start | bytes 497668
  40.8 0.9 %copy-start.13 = (bf16[192,288]{1,0:T(8,128)(2,1)S(1)}, bf16[192,288]{1,0:T(8,128)(2,1)}, u32[]{:S(2)}) copy-start(bf16[192,288]{1,0:T(8,128)(2,1)} %copy-done.12) | copy-start | bytes 331780
  44.1 3.5 %collective-permute-start.10 = (bf16[128,288]{1,0:T(8,128)(2,1)S(1)}, bf16[128,288]{1,0:T(8,128)(2,1)S(1)}, u32[]{:S(2)}, u32[]{:S(2)}) collective-permute-start(bf16[128,288]{1,0:T(8,128)(2,1)S(1)} %get-tuple-element.34), channel_id=1, source_target_pairs={{0,2},{1,3},{2,0},{3,1},{4,6},{5,7},{6,4},{7,5},{8,10},{9,11},{10,... | collective-permute-start | bytes 221192 | tf_op jit(solution)/shard_map/ppermute | solution.py:48
  44.5 4.4 %collective-permute-start.11 = (bf16[128,288]{1,0:T(8,128)(2,1)S(1)}, bf16[128,288]{1,0:T(8,128)(2,1)S(1)}, u32[]{:S(2)}, u32[]{:S(2)}) collective-permute-start(bf16[128,288]{1,0:T(8,128)(2,1)S(1)} %get-tuple-element.34), channel_id=1, source_target_pairs={{0,3},{1,2},{2,1},{3,0},{4,7},{5,6},{6,5},{7,4},{8,11},{9,10},{10,... | collective-permute-start | bytes 221192 | tf_op jit(solution)/shard_map/ppermute | solution.py:48
  45.5 4.3 %collective-permute-start.9 = (bf16[128,288]{1,0:T(8,128)(2,1)S(1)}, bf16[128,288]{1,0:T(8,128)(2,1)S(1)}, u32[]{:S(2)}, u32[]{:S(2)}) collective-permute-start(bf16[128,288]{1,0:T(8,128)(2,1)S(1)} %get-tuple-element.34), channel_id=1, source_target_pairs={{0,1},{1,0},{2,3},{3,2},{4,5},{5,4},{6,7},{7,6},{8,9},{9,8},{10,11... | collective-permute-start | bytes 221192 | tf_op jit(solution)/shard_map/ppermute | solution.py:48
  49.8 1.8 %copy-start.1 = (bf16[1,1,1152,1152]{3,2,1,0:T(8,128)(2,1)S(1)}, bf16[1,1,1152,1152]{3,2,1,0:T(8,128)(2,1)}, u32[]{:S(2)}) copy-start(bf16[1,1,1152,1152]{3,2,1,0:T(8,128)(2,1)} %param.21) | copy-start | bytes 7962628
  51.6 13.8 %copy-start.16 = (bf16[1152,16]{0,1:T(8,128)(2,1)S(1)}, bf16[1152,16]{0,1:T(8,128)(2,1)}, u32[]{:S(2)}) copy-start(bf16[1152,16]{0,1:T(8,128)(2,1)} %param.22) | copy-start | bytes 110596
  51.6 15.4 %copy-start.14 = (f32[1,2,1152]{2,1,0:T(2,128)S(1)}, f32[1,2,1152]{2,1,0:T(2,128)}, u32[]{:S(2)}) copy-start(f32[1,2,1152]{2,1,0:T(2,128)} %param.17) | copy-start | bytes 27652
  51.6 15.4 %copy-start.15 = (f32[1,256]{1,0:T(1,128)S(1)}, f32[1,256]{1,0:T(1,128)}, u32[]{:S(2)}) copy-start(f32[1,256]{1,0:T(1,128)} %noisy.1) | copy-start | bytes 3076
  53.2 3.3 %collective-permute-start.12 = (bf16[32,1152]{1,0:T(8,128)(2,1)S(1)}, bf16[32,1152]{1,0:T(8,128)(2,1)S(1)}, u32[]{:S(2)}, u32[]{:S(2)}) collective-permute-start(bf16[32,1152]{1,0:T(8,128)(2,1)S(1)} %get-tuple-element.36), channel_id=1, source_target_pairs={{0,1},{1,0},{2,3},{3,2},{4,5},{5,4},{6,7},{7,6},{8,9},{9,8},{10,11... | collective-permute-start | bytes 221192 | tf_op jit(solution)/shard_map/ppermute | solution.py:48
  53.7 3.2 %collective-permute-start.13 = (bf16[32,1152]{1,0:T(8,128)(2,1)S(1)}, bf16[32,1152]{1,0:T(8,128)(2,1)S(1)}, u32[]{:S(2)}, u32[]{:S(2)}) collective-permute-start(bf16[32,1152]{1,0:T(8,128)(2,1)S(1)} %get-tuple-element.37), channel_id=1, source_target_pairs={{0,2},{1,3},{2,0},{3,1},{4,6},{5,7},{6,4},{7,5},{8,10},{9,11},{10,... | collective-permute-start | bytes 221192 | tf_op jit(solution)/shard_map/ppermute | solution.py:48
  54.7 4.1 %collective-permute-start.14 = (bf16[32,1152]{1,0:T(8,128)(2,1)S(1)}, bf16[32,1152]{1,0:T(8,128)(2,1)S(1)}, u32[]{:S(2)}, u32[]{:S(2)}) collective-permute-start(bf16[32,1152]{1,0:T(8,128)(2,1)S(1)} %get-tuple-element.38), channel_id=1, source_target_pairs={{0,3},{1,2},{2,1},{3,0},{4,7},{5,6},{6,5},{7,4},{8,11},{9,10},{10,... | collective-permute-start | bytes 221192 | tf_op jit(solution)/shard_map/ppermute | solution.py:48
  58.9 8.1 %collective-permute-start.15 = (bf16[16,1152]{1,0:T(8,128)(2,1)S(1)}, bf16[16,1152]{1,0:T(8,128)(2,1)S(1)}, u32[]{:S(2)}, u32[]{:S(2)}) collective-permute-start(bf16[16,1152]{1,0:T(8,128)(2,1)S(1)} %get-tuple-element.40), channel_id=1, source_target_pairs={{0,16},{16,0},{1,17},{17,1},{2,18},{18,2},{3,19},{19,3},{4,20},{20... | collective-permute-start | bytes 110600 | tf_op jit(solution)/shard_map/ppermute | solution.py:309
  (1 other events, 0.7 us)

commit v2 on v0

v2 whole, which is shorter than its diff:
```python
from functools import partial

import jax
import jax.numpy as jnp
from jax import lax
from jax.experimental import pallas as pl
from jax.experimental.pallas import tpu as pltpu
from jax.sharding import PartitionSpec as P

HEADS = 16
UNIT_GROUPS = 4


NORM_EPS = 1e-06
BETA_LOW = 0.0001
BETA_HIGH = 0.02

ORDER = tuple(reversed(range(UNIT_GROUPS)))

BF16 = jnp.bfloat16
F32 = jnp.float32
VMEM = pl.BlockSpec(memory_space=pltpu.VMEM)
HBM = pl.BlockSpec(memory_space=pltpu.HBM)
PARAMS = pltpu.CompilerParams(vmem_limit_bytes=12 * 1024 * 1024)


def layer_norm(values):
    average = jnp.mean(values, axis=-1, keepdims=True)
    centred = values - average
    spread = jnp.mean(centred * centred, axis=-1, keepdims=True)
    return centred * lax.rsqrt(spread + NORM_EPS)


def alpha_bar(moment):
    return jnp.exp(
        -(BETA_LOW * (moment + 1.0) + (BETA_HIGH - BETA_LOW) * moment * (moment + 1.0) / 1998.0)
    )


def own_block():
    return lax.rem(lax.axis_index("req"), UNIT_GROUPS)


def other_block(block, k):
    return lax.bitwise_xor(block, jnp.int32(k))


def swap(x, k):
    return lax.ppermute(x, "req", [(i, i ^ k) for i in range(lax.axis_size("req"))])


def swap_each(arrays):
    return [swap(array, k) if k else array for k, array in zip(ORDER, arrays)][::-1]


def call(body, outs, *args, far=(), scratch=(), micros=0.0, turn=True):
    specs = [HBM if i in far else VMEM for i in range(len(args))]
    args = [pltpu.with_memory_space_constraint(arg, pltpu.HBM) if i in far else arg for i, arg in enumerate(args)]
    way = -1 if turn else 1

    def turned(*refs):
        body(*refs[: len(args)][::way], *refs[len(args) :])

    return pl.pallas_call(
        turned,
        out_shape=outs,
        in_specs=specs[::way],
        out_specs=jax.tree.map(lambda _: VMEM, outs),
        scratch_shapes=list(scratch),
        compiler_params=PARAMS,
        cost_estimate=pl.CostEstimate(flops=int(micros * 1e9), bytes_accessed=0, transcendentals=0),
        name=body.__name__,
    )(*args[::way])


def cut(rows, count):
    part = rows.shape[1] // count
    return [rows[:, i * part : (i + 1) * part] for i in range(count)]


def beside(pieces):
    return jnp.concatenate(pieces, axis=1)


def below(pieces):
    return jnp.concatenate(pieces, axis=0)


def product(left, right_rows):
    return lax.dot_general(left, right_rows, (((1,), (1,)), ((), ())), preferred_element_type=F32)


MOD_ROWS = (0, 1, 2, 3, 4)
LOW_ROWS = (1, 2, 4)


def gather_kernel(hidden_far, mods_far, stale_far, packed, mods, stale, sems):
    fresh = hidden_far.shape[0]
    copies = [
        pltpu.make_async_copy(mods_far, mods, sems.at[0]),
        pltpu.make_async_copy(hidden_far, packed.at[pl.ds(0, fresh)], sems.at[1]),
        pltpu.make_async_copy(stale_far, stale, sems.at[2]),
    ]
    for copy in copies:
        copy.start()
    copies[0].wait()
    rows = [mods[i] for i in MOD_ROWS] + [mods[i] - mods[i].astype(BF16).astype(F32) for i in LOW_ROWS]
    packed[fresh:, :] = below(rows).astype(BF16)
    copies[1].wait()
    copies[2].wait()


def mod_row(packed, i):
    first = packed.shape[0] - len(MOD_ROWS) - len(LOW_ROWS)
    rows = packed[first:, :].astype(F32)
    row = rows[i : i + 1]
    if i in LOW_ROWS:
        at = len(MOD_ROWS) + LOW_ROWS.index(i)
        row = row + rows[at : at + 1]
    return row


def token_rows(packed):
    return packed[: packed.shape[0] - len(MOD_ROWS) - len(LOW_ROWS), :]


def factor_kernel(now, gap, factors):
    columns = factors.shape[1]
    now_bar = alpha_bar(jnp.broadcast_to(now[...], (1, columns)).astype(F32))
    prev_bar = alpha_bar(jnp.broadcast_to(now[...] - gap[...], (1, columns)).astype(F32))
    factors[0:1, :] = jnp.sqrt(1.0 - now_bar)
    factors[1:2, :] = jnp.sqrt(now_bar)
    factors[2:3, :] = jnp.sqrt(1.0 - prev_bar)
    factors[3:4, :] = jnp.sqrt(prev_bar)


def pack_kernel(stale, patch, *rest):
    *outs, packed = rest
    width = stale.shape[1] // 2
    part = width // UNIT_GROUPS
    fresh = 2 * outs[0].shape[0] // 3
    patches = stale.shape[0] // fresh
    at = patch[...]
    keys_values = [stale[i * fresh : (i + 1) * fresh, :] for i in range(patches)]
    kept = []
    for i in range(1, patches):
        rows = keys_values[i]
        for start in range(1, patches):
            rows = jnp.where(at == start, keys_values[(start + i) % patches], rows)
        kept.append(rows)
    keys = [cut(rows[:, :width], UNIT_GROUPS) for rows in kept]
    values = [cut(rows[:, width:], UNIT_GROUPS) for rows in kept]
    for block in range(UNIT_GROUPS):
        first = [rows[block] for rows in keys] + [values[0][block]]
        second = beside([rows[block] for rows in values[1:]])
        packed[block, :fresh, :] = beside(first)
        packed[block, fresh:, :] = beside([second[: fresh // 2], second[fresh // 2 :]])
    here = own_block()
    for k, out in zip(ORDER, outs):
        out[...] = packed[other_block(here, k)]


def unpack(packed):
    fresh = 2 * packed.shape[0] // 3
    first = cut(packed[:fresh, :], UNIT_GROUPS)
    second = cut(below(cut(packed[fresh:, :], 2)), 2)
    return first[:3], first[3:] + second


def join_kernel(t0, t1, t2, t3, weight, queries, keys, values, near, second, own):
    tokens = []
    for packed in (t0, t1, t2, t3):
        rows = layer_norm(token_rows(packed).astype(F32))
        tokens.append((rows * (1.0 + mod_row(packed, 1)) + mod_row(packed, 0)).astype(BF16))
    fresh = tokens[0].shape[0]
    joined = product(below(tokens), weight[...]).astype(BF16)
    q, k, v = cut(joined, 3)
    part = q.shape[1]
    heads = HEADS // UNIT_GROUPS
    inside = head_lanes(fresh, part)
    zero = jnp.zeros((fresh, part), BF16)
    for m in range(UNIT_GROUPS):
        rows = q[m * fresh : (m + 1) * fresh]
        for h in range(heads):
            at = (m * heads + h) * fresh
            queries[at : at + fresh, :] = jnp.where(inside[h], rows, zero)
    keys[...] = k
    values[...] = v
    pairs = [joined[m * fresh : (m + 1) * fresh, part:] for m in range(UNIT_GROUPS)]
    near[...] = beside([pairs[1], pairs[3]])
    second[...] = pairs[2]
    own[...] = pairs[0]


def head_lanes(rows, part):
    heads = HEADS // UNIT_GROUPS
    head_size = part // heads
    lane = lax.broadcasted_iota(jnp.int32, (rows, part), 1)
    return [(lane >= h * head_size) & (lane < (h + 1) * head_size) for h in range(heads)]


def attend_kernel(queries, k, v, p0, p1, p2, p3, sent):
    count, part = k.shape
    fresh = count // UNIT_GROUPS
    heads = HEADS // UNIT_GROUPS
    inside = head_lanes(fresh, part)
    scores = []
    values = []
    for m, packed in enumerate((p0, p1, p2, p3)):
        rows = slice(m * fresh, (m + 1) * fresh)
        stale_keys, stale_values = unpack(packed)
        spread = queries[m * heads * fresh : (m + 1) * heads * fresh, :]
        scores.append(product(spread, below(stale_keys + [k[rows, :]])))
        values.append(below(stale_values + [v[rows, :]]))
    scores = below(scores) * (part // heads) ** (-0.5)
    raised = jnp.exp(scores - jnp.max(scores, axis=-1, keepdims=True))
    probs = (raised * (1.0 / jnp.sum(raised, axis=-1, keepdims=True))).astype(BF16)
    mixed = []
    for m in range(UNIT_GROUPS):
        found = jnp.dot(probs[m * heads * fresh : (m + 1) * heads * fresh], values[m], preferred_element_type=F32)
        total = jnp.where(inside[0], found[:fresh], 0.0)
        for h in range(1, heads):
            total = jnp.where(inside[h], found[h * fresh : (h + 1) * fresh], total)
        mixed.append(total.astype(BF16))
    sent[...] = beside(mixed)


def place_blocks(columns, pieces):
    here = own_block()
    for k, piece in enumerate(pieces):
        slots = cut(piece[...], UNIT_GROUPS)
        columns[other_block(here, k)] = below([slots[k ^ m] for m in range(UNIT_GROUPS)])
    return beside([columns[block] for block in range(UNIT_GROUPS)])


def project_kernel(a0, a1, a2, a3, weight, near, sent, onward, columns):
    projected = product(place_blocks(columns, (a0, a1, a2, a3)), weight[...]).astype(BF16)
    fresh = sent.shape[0]
    onward[...] = near[...]
    sent[...] = beside([projected[m * fresh : (m + 1) * fresh] for m in range(UNIT_GROUPS)])


def relay_kernel(second, arrived, onward):
    onward[...] = beside([second[...], cut(arrived[...], 2)[1]])


def fresh_kernel(own, near, far, fresh_kv, columns):
    here = own_block()
    for k, rows in enumerate((own[...], cut(near[...], 2)[0], *cut(far[...], 2))):
        columns[other_block(here, k)] = rows
    pairs = [cut(columns[block], 2) for block in range(UNIT_GROUPS)]
    fresh_kv[...] = beside([pair[0] for pair in pairs] + [pair[1] for pair in pairs])


def mlp_kernel(h0, h1, h2, h3, t0, t1, t2, t3, w_up, w_down, *rest):
    *outs, home, columns = rest
    fresh = h0.shape[0]
    projected = place_blocks(columns, (h0, h1, h2, h3)).astype(F32)
    middle = []
    for m, packed in enumerate((t0, t1, t2, t3)):
        gated = mod_row(packed, 2) * projected[m * fresh : (m + 1) * fresh]
        values = token_rows(packed).astype(F32) + gated
        if m == 0:
            home[...] = values
        middle.append((layer_norm(values) * (1.0 + mod_row(packed, 4)) + mod_row(packed, 3)).astype(BF16))
    middle = below(middle)
    inner = jnp.dot(middle, w_up[...], preferred_element_type=F32)
    inner = jax.nn.gelu(inner, approximate=True).astype(BF16)
    partial_out = jnp.dot(inner, w_down[...], preferred_element_type=F32)
    for m, out in zip(ORDER, outs):
        out[...] = partial_out[m * fresh : (m + 1) * fresh].astype(BF16)


def total_kernel(o0, o1, o2, o3, home, mods, last_mods, weight, kept, noise, sent):
    half = kept.shape[0]
    section = lax.axis_index("section")
    columns = noise.shape[1]
    found = []
    for at in (section, 1 - section):
        rows = pl.ds(pl.multiple_of(at * half, half), half)
        total = (o0[rows, :].astype(F32) + o1[rows, :].astype(F32)) + (
            o2[rows, :].astype(F32) + o3[rows, :].astype(F32)
        )
        found.append((home[rows, :] + mods[5] * total).astype(BF16))
    kept[...] = found[0]
    sent[:half, :] = found[1]

    @pl.when(section == 1)
    def _():
        rows = below(found).astype(F32)
        shifted = (layer_norm(rows) * (1.0 + last_mods[1:2, :]) + last_mods[0:1, :]).astype(BF16)
        repeated = product(shifted, weight[...])
        channels = columns // half
        lane = lax.broadcasted_iota(jnp.int32, (half, columns), 1)
        token = lax.broadcasted_iota(jnp.int32, (half, columns), 0)
        mine = (lane >= token * channels) & (lane < (token + 1) * channels)
        own, other = [
            jnp.sum(jnp.where(mine, rows, 0.0), axis=0, keepdims=True) for rows in (repeated[:half], repeated[half:])
        ]
        noise[...] = own
        parts = []
        for _ in range(3):
            parts.append(other.astype(BF16).astype(F32))
            other = other - parts[-1]
        blank = jnp.zeros((sent.shape[0] - half - len(parts), columns), F32)
        sent[half:, :columns] = below(parts + [blank]).astype(BF16)


def final_kernel(factors, kept, arrived, own_noise, noisy, next_rows, noise, denoised):
    first = lax.axis_index("section") == 0
    half, columns = kept.shape[0], noise.shape[1]
    next_rows[...] = jnp.where(first, kept[...], arrived[:half, :])
    parts = arrived[half:, :columns].astype(F32)
    value = jnp.where(first, parts[0:1] + parts[1:2] + parts[2:3], own_noise[...])
    noise[...] = value
    clean = (noisy[...] - factors[0:1, :] * value) / factors[1:2, :]
    denoised[...] = factors[3:4, :] * clean + factors[2:3, :] * value


def per_device(
    section_in,
    patch_index,
    stale_kv,
    modulation,
    final_mod,
    qkv_blocks,
    out_blocks,
    up_blocks,
    down_blocks,
    final_weight,
    noisy_latent,
    time_index,
    time_gap,
):
    shape = jax.ShapeDtypeStruct
    hidden, stale = section_in[0, 0], stale_kv[0, 0]
    mods = modulation[0, 0][:, None, :]
    fresh, width = hidden.shape
    part = width // UNIT_GROUPS
    half = fresh // 2
    count = UNIT_GROUPS * fresh
    others = range(1, UNIT_GROUPS)

    packed, mods, stale = call(
        gather_kernel,
        [
            shape((fresh + len(MOD_ROWS) + len(LOW_ROWS), width), BF16),
            shape(mods.shape, F32),
            shape(stale.shape, BF16),
        ],
        hidden,
        mods,
        stale,
        far=range(3),
        scratch=[pltpu.SemaphoreType.DMA((3,))],
        micros=1.0,
    )
    slots = [packed] + [swap(packed, k) for k in others]
    pack_rows = fresh + fresh // 2
    packs = call(
        pack_kernel,
        [shape((pack_rows, width), BF16)] * UNIT_GROUPS,
        stale,
        patch_index,
        scratch=[pltpu.VMEM((UNIT_GROUPS, pack_rows, width), BF16)],
        micros=6.0,
    )
    factors = call(
        factor_kernel,
        shape((8, noisy_latent.shape[1]), F32),
        time_index[None],
        time_gap[None],
        micros=1.0,
    )
    packs = swap_each(packs)
    w_qkv = qkv_blocks[0, 0].T
    queries, keys, values, near, second, own = call(
        join_kernel,
        [
            shape((HEADS // UNIT_GROUPS * count, part), BF16),
            shape((count, part), BF16),
            shape((count, part), BF16),
            shape((fresh, width), BF16),
            shape((fresh, 2 * part), BF16),
            shape((fresh, 2 * part), BF16),
        ],
        *slots,
        w_qkv,
        micros=1.0,
    )
    sent = call(attend_kernel, shape((fresh, width), BF16), queries, keys, values, *packs, micros=2.0)
    mixed = [sent] + [swap(sent, k) for k in others]
    sent, near = call(
        project_kernel,
        [shape((fresh, width), BF16)] * 2,
        *mixed,
        out_blocks[0, 0].T,
        near,
        scratch=[pltpu.VMEM((UNIT_GROUPS, count, part), BF16)],
        micros=1.0,
    )
    pieces = [sent] + [swap(sent, k) for k in others]
    near = swap(near, 1)
    onward = call(relay_kernel, shape((fresh, width), BF16), second, near, micros=0.1)
    fresh_kv = call(
        fresh_kernel,
        shape((fresh, 2 * width), BF16),
        own,
        near,
        swap(onward, 2),
        scratch=[pltpu.VMEM((UNIT_GROUPS, fresh, 2 * part), BF16)],
        micros=1.0,
    )
    *parts, home = call(
        mlp_kernel,
        [shape((fresh, width), BF16)] * UNIT_GROUPS + [shape((fresh, width), F32)],
        *pieces,
        *slots,
        up_blocks[0, 0],
        down_blocks[0, 0],
        scratch=[pltpu.VMEM((UNIT_GROUPS, count, part), BF16)],
        micros=2.0,
    )
    parts = swap_each(parts)
    row = shape(noisy_latent.shape, F32)
    kept, own_noise, sent = call(
        total_kernel,
        [shape((half, width), BF16), row, shape((half + 16, width), BF16)],
        *parts,
        home,
        mods,
        final_mod[0],
        jnp.tile(final_weight.T, (half, 1)),
    )
    next_rows, noise, denoised = call(
        final_kernel,
        [shape((half, width), BF16), row, row],
        factors,
        kept,
        lax.ppermute(sent, "section", [(0, 1), (1, 0)]),
        own_noise,
        noisy_latent,
    )
    return (fresh_kv[None, None], next_rows[None], noise, denoised)


def solution(mesh):
    placed = (
        P("section", "req", None, None),
        P("section", "req"),
        P("section", "req", None, None),
        P("section", "req", None, None),
        P("req", None, None),
        P("section", "req", None, None),
        P("section", "req", None, None),
        P("section", "req", None, None),
        P("section", "req", None, None),
        P(),
        P("req", "section"),
        P("req"),
        P("req"),
    )
    return jax.shard_map(
        per_device,
        mesh=mesh,
        in_specs=placed,
        out_specs=(
            P("section", "req", None, None),
            P("req", "section", None),
            P("req", "section"),
            P("req", "section"),
        ),
        check_vma=False,
    )
```

time: 109 us -> 42.7 us (0.39)
  blocking collectives: 50.2 us -> 0 us
  matrix products: 10.9 us -> 0 us
  local copies, waits for them, and re-layouts: 9.11 us -> 0.08 us
  starting transfers between devices: 13.7 us -> 22.2 us
  Pallas kernels: 0 us -> 8.3 us
  other arithmetic: 6.87 us -> 0 us
  waiting for transfers between devices: 14.1 us -> 8.79 us
    all_to_all x4 -> x0, blocking collectives: 50.2 us -> none  [the longest x3 38.4 us: spread_regroup(): lax.all_to_all(outgoing, 'req', split_axis=0, concat_axis=0, tiled=True)]
    ppermute x1 -> x18, starting transfers between devices: 5.21 us -> 22.2 us  [the longest x17 17 us: swap(): lax.ppermute(x, 'req', [(i, i ^ k) for i in range(lax.axis_size('req'))])]
    all_to_all x2 -> x0, waiting for transfers between devices: 14.1 us -> none  [spread_regroup(): lax.all_to_all(block_fn(lax.all_to_all(outgoing, 'req', split_axis=0, con...]
    dot_general x6 -> x0, matrix products: 10.9 us -> none  [the longest x2 4.46 us: block_product(): jnp.einsum('nsd,dc->nsc', incoming, weight, preferred_element_type=jnp.fl...]
    ppermute x1 -> x18, waiting for transfers between devices: 0.01 us -> 8.79 us  [the longest x17 8.73 us: swap(): lax.ppermute(x, 'req', [(i, i ^ k) for i in range(lax.axis_size('req'))])]
    all_to_all x2 -> x0, starting transfers between devices: 8.46 us -> none  [spread_regroup(): lax.all_to_all(block_fn(lax.all_to_all(outgoing, 'req', split_axis=0, con...]
    pallas_call x0 -> x11, Pallas kernels: none -> 8.3 us  [call(): pl.pallas_call(turned, out_shape=outs, in_specs=specs[::way], out_specs=j...]
    reduce_sum x7 -> x0, other arithmetic: 2.77 us -> none  [the longest x3 1.47 us: layer_norm(): spread = jnp.mean(centred * centred, axis=-1, keepdims=True)]
  transfers between devices with their start and end apart: 3 -> 18, of which waited for: 2 -> 11; matrix products, arithmetic and copies ran while one was open for 0% -> 0% of each run, Pallas kernels for 0% -> 11%
where the time goes in v2:
time: 42.7 us; the launch traced here: 42.1 us
  starting transfers between devices  22.2 us (52%)
  waiting for transfers between devices  8.79 us (21%)
  Pallas kernels  8.3 us (19%)
  between operations  2.71 us (6%)
    ppermute x17, starting transfers between devices, swap(): lax.ppermute(x, 'req', [(i, i ^ k) for i in range(lax.axis_size('req'))])  17 us
    ppermute x17, waiting for transfers between devices, swap(): lax.ppermute(x, 'req', [(i, i ^ k) for i in range(lax.axis_size('req'))])  8.73 us
    pallas_call x11, Pallas kernels, call(): pl.pallas_call(turned, out_shape=outs, in_specs=specs[::way], out_specs=j...  8.3 us
    ppermute x1, starting transfers between devices, per_device(): lax.ppermute(sent, 'section', [(0, 1), (1, 0)])  5.22 us
  transfers between devices with their start and end apart: 18, of which 11 were waited for; matrix products, arithmetic and copies ran while one was open for 0% of the time, Pallas kernels for 11%

profile of v2, /device:TPU:1, one launch (start us, length us, event | category | flops | bytes accessed | tf_op | source)
XLA Modules:
  0.0 42.1 jit_solution(7931819512787465866)
XLA Ops:
  0.6 1.2 %gather_kernel.1 = (bf16[40,1152]{1,0:T(8,128)(2,1)S(1)}, f32[6,1,1152]{2,1,0:T(1,128)S(1)}, bf16[128,2304]{1,0:T(8,128)(2,1)S(1)}) custom-call(bf16[128,2304]{1,0:T(8,128)(2,1)} %bitcast.27, f32[6,1,1152]{2,1,0:T(1,128)} %bitcast.30, bf16[32,1152]{1,0:T(8,128)(2,1)} %bitcast.28), custom_call_target="tpu_custom_call" | custom-call | flops 1000000000 | tf_op jit(solution)/shard_map/gather_kernel/pallas_call | solution.py:64
  1.8 3.1 %collective-permute-start = (bf16[40,1152]{1,0:T(8,128)(2,1)S(1)}, bf16[40,1152]{1,0:T(8,128)(2,1)S(1)}, u32[]{:S(2)}, u32[]{:S(2)}) collective-permute-start(bf16[40,1152]{1,0:T(8,128)(2,1)S(1)} %get-tuple-element.30.refs_4_.refs_5_), channel_id=1, source_target_pairs={{0,3},{1,2},{2,1},{3,0},{4,7},{5,6},{6,5},{7,4},{8,11},{9,10},{10,... | collective-permute-start | bytes 276488 | tf_op jit(solution)/shard_map/ppermute | solution.py:49
  4.9 0.2 collective-permute-start.1
  5.9 0.3 pack_kernel.1
  6.2 2.4 %collective-permute-start.3 = (bf16[48,1152]{1,0:T(8,128)(2,1)S(1)}, bf16[48,1152]{1,0:T(8,128)(2,1)S(1)}, u32[]{:S(2)}, u32[]{:S(2)}) collective-permute-start(bf16[48,1152]{1,0:T(8,128)(2,1)S(1)} %get-tuple-element.33), channel_id=1, source_target_pairs={{0,3},{1,2},{2,1},{3,0},{4,7},{5,6},{6,5},{7,4},{8,11},{9,10},{10,... | collective-permute-start | bytes 331784 | tf_op jit(solution)/shard_map/ppermute | solution.py:49
  9.1 0.4 collective-permute-done.2.refs_3_.refs_4_
  9.5 1.1 %join_kernel.1 = (bf16[512,288]{1,0:T(8,128)(2,1)S(1)}, bf16[128,288]{1,0:T(8,128)(2,1)S(1)}, bf16[128,288]{1,0:T(8,128)(2,1)S(1)}, bf16[32,1152]{1,0:T(8,128)(2...) custom-call(bf16[864,1152]{1,0:T(8,128)(2,1)S(1)} %bitcast.24, ...), custom_call_target="tpu_custom_call" | custom-call | flops 1000000000 | tf_op jit(solution)/shard_map/join_kernel/pallas_call | solution.py:64
  10.5 0.9 %collective-permute-done.3.refs_0_ = bf16[48,1152]{1,0:T(8,128)(2,1)S(1)} collective-permute-done((bf16[48,1152]{1,0:T(8,128)(2,1)S(1)}, bf16[48,1152]{1,0:T(8,128)(2,1)S(1)}, u32[]{:S(2)}, u32[]{:S(2)}) %collective-permute-start.3) | collective-permute-done | bytes 110624 | tf_op jit(solution)/shard_map/ppermute | solution.py:49
  11.5 2.5 %collective-permute-done.4.refs_1_ = bf16[48,1152]{1,0:T(8,128)(2,1)S(1)} collective-permute-done((bf16[48,1152]{1,0:T(8,128)(2,1)S(1)}, bf16[48,1152]{1,0:T(8,128)(2,1)S(1)}, u32[]{:S(2)}, u32[]{:S(2)}) %collective-permute-start.4) | collective-permute-done | bytes 110624 | tf_op jit(solution)/shard_map/ppermute | solution.py:49
  14.0 1.3 %attend_kernel.1.refs_5_ = bf16[32,1152]{1,0:T(8,128)(2,1)S(1)} custom-call(bf16[48,1152]{1,0:T(8,128)(2,1)S(1)} %collective-permute-done.3.refs_0_, bf16[48,1152]{1,0:T(8,128)(2,1)S(1)} %collective-permute-done.4.refs_1_, bf16[48,1152]{1,0:T(8,128)(2,1)S(1)} %collective-permute-done.5.refs_2_, bf16[48,1152]{1,0:T(8,128)(2,1)S(1)} %get-tuple-element.36.refs_3_, ...), custom_call_target="tpu_custom_call" | custom-call | flops 2000000000 | tf_op jit(solution)/shard_map/attend_kernel/pallas_call | solution.py:64
  15.3 0.9 %collective-permute-start.6 = (bf16[32,1152]{1,0:T(8,128)(2,1)S(1)}, bf16[32,1152]{1,0:T(8,128)(2,1)S(1)}, u32[]{:S(2)}, u32[]{:S(2)}) collective-permute-start(bf16[32,1152]{1,0:T(8,128)(2,1)S(1)} %attend_kernel.1.refs_5_), channel_id=1, source_target_pairs={{0,3},{1,2},{2,1},{3,0},{4,7},{5,6},{6,5},{7,4},{8,11},{9,10},{10,... | collective-permute-start | bytes 221192 | tf_op jit(solution)/shard_map/ppermute | solution.py:49
  16.2 1.3 %collective-permute-start.7 = (bf16[32,1152]{1,0:T(8,128)(2,1)S(1)}, bf16[32,1152]{1,0:T(8,128)(2,1)S(1)}, u32[]{:S(2)}, u32[]{:S(2)}) collective-permute-start(bf16[32,1152]{1,0:T(8,128)(2,1)S(1)} %attend_kernel.1.refs_5_), channel_id=1, source_target_pairs={{0,2},{1,3},{2,0},{3,1},{4,6},{5,7},{6,4},{7,5},{8,10},{9,11},{10,... | collective-permute-start | bytes 221192 | tf_op jit(solution)/shard_map/ppermute | solution.py:49
  17.5 0.5 %collective-permute-start.8 = (bf16[32,1152]{1,0:T(8,128)(2,1)S(1)}, bf16[32,1152]{1,0:T(8,128)(2,1)S(1)}, u32[]{:S(2)}, u32[]{:S(2)}) collective-permute-start(bf16[32,1152]{1,0:T(8,128)(2,1)S(1)} %attend_kernel.1.refs_5_), channel_id=1, source_target_pairs={{0,1},{1,0},{2,3},{3,2},{4,5},{5,4},{6,7},{7,6},{8,9},{9,8},{10,11... | collective-permute-start | bytes 221192 | tf_op jit(solution)/shard_map/ppermute | solution.py:49
  18.0 1.5 %collective-permute-done.6.refs_2_ = bf16[32,1152]{1,0:T(8,128)(2,1)S(1)} collective-permute-done((bf16[32,1152]{1,0:T(8,128)(2,1)S(1)}, bf16[32,1152]{1,0:T(8,128)(2,1)S(1)}, u32[]{:S(2)}, u32[]{:S(2)}) %collective-permute-start.6) | collective-permute-done | bytes 73760 | tf_op jit(solution)/shard_map/ppermute | solution.py:49
  19.5 0.7 %collective-permute-done.7.refs_3_ = bf16[32,1152]{1,0:T(8,128)(2,1)S(1)} collective-permute-done((bf16[32,1152]{1,0:T(8,128)(2,1)S(1)}, bf16[32,1152]{1,0:T(8,128)(2,1)S(1)}, u32[]{:S(2)}, u32[]{:S(2)}) %collective-permute-start.7) | collective-permute-done | bytes 73760 | tf_op jit(solution)/shard_map/ppermute | solution.py:49
  20.2 0.5 %collective-permute-done.8.refs_4_ = bf16[32,1152]{1,0:T(8,128)(2,1)S(1)} collective-permute-done((bf16[32,1152]{1,0:T(8,128)(2,1)S(1)}, bf16[32,1152]{1,0:T(8,128)(2,1)S(1)}, u32[]{:S(2)}, u32[]{:S(2)}) %collective-permute-start.8) | collective-permute-done | bytes 73760 | tf_op jit(solution)/shard_map/ppermute | solution.py:49
  20.7 0.7 %project_kernel.1 = (bf16[32,1152]{1,0:T(8,128)(2,1)S(1)}, bf16[32,1152]{1,0:T(8,128)(2,1)S(1)}) custom-call(bf16[32,1152]{1,0:T(8,128)(2,1)S(1)} %get-tuple-element.31.refs_0_, bf16[288,1152]{1,0:T(8,128)(2,1)S(1)} %bitcast.25, bf16[32,1152]{1,0:T(8,128)(2,1)S(1)} %collective-permute-done.6.refs_2_, bf16[32,1152]{1,0:T(8,128)(2,1)S(1)} %collective-permute-done.7.refs_3_, ...), custom_call_target="tpu_custom_call" | custom-call | flops 1000000000 | tf_op jit(solution)/shard_map/project_kernel/pallas_call | solution.py:64
  21.5 2.4 %collective-permute-start.11 = (bf16[32,1152]{1,0:T(8,128)(2,1)S(1)}, bf16[32,1152]{1,0:T(8,128)(2,1)S(1)}, u32[]{:S(2)}, u32[]{:S(2)}) collective-permute-start(bf16[32,1152]{1,0:T(8,128)(2,1)S(1)} %get-tuple-element.44.refs_9_), channel_id=1, source_target_pairs={{0,3},{1,2},{2,1},{3,0},{4,7},{5,6},{6,5},{7,4},{8,11},{9,10},{10,... | collective-permute-start | bytes 221192 | tf_op jit(solution)/shard_map/ppermute | solution.py:49
  23.9 0.4 collective-permute-start.13
  25.5 1.2 %collective-permute-start.9 = (bf16[32,1152]{1,0:T(8,128)(2,1)S(1)}, bf16[32,1152]{1,0:T(8,128)(2,1)S(1)}, u32[]{:S(2)}, u32[]{:S(2)}) collective-permute-start(bf16[32,1152]{1,0:T(8,128)(2,1)S(1)} %get-tuple-element.40), channel_id=1, source_target_pairs={{0,1},{1,0},{2,3},{3,2},{4,5},{5,4},{6,7},{7,6},{8,9},{9,8},{10,11... | collective-permute-start | bytes 221192 | tf_op jit(solution)/shard_map/ppermute | solution.py:49
  26.7 0.4 collective-permute-done.12.refs_7_
  27.1 1.6 %mlp_kernel.1 = (bf16[32,1152]{1,0:T(8,128)(2,1)S(1)}, bf16[32,1152]{1,0:T(8,128)(2,1)S(1)}, bf16[32,1152]{1,0:T(8,128)(2,1)S(1)}, bf16[32,1152]{1,0:T(8,128)(2,1)S(1)}, f32[32,1152]{1,0:T(8,128)S(1)}) custom-call(bf16[1152,1152]{1,0:T(8,128)(2,1)S(1)} %bitcast.22, bf16[1152,1152]{1,0:T(8,128)(2,1)S(1)} %bitcast.23, ...), custom_call_target="tpu_custom_call" | custom-call | flops 2000000000 | tf_op jit(solution)/shard_map/mlp_kernel/pallas_call | solution.py:64
  28.7 1.2 %collective-permute-start.14 = (bf16[32,1152]{1,0:T(8,128)(2,1)S(1)}, bf16[32,1152]{1,0:T(8,128)(2,1)S(1)}, u32[]{:S(2)}, u32[]{:S(2)}) collective-permute-start(bf16[32,1152]{1,0:T(8,128)(2,1)S(1)} %get-tuple-element.46), channel_id=1, source_target_pairs={{0,3},{1,2},{2,1},{3,0},{4,7},{5,6},{6,5},{7,4},{8,11},{9,10},{10,... | collective-permute-start | bytes 221192 | tf_op jit(solution)/shard_map/ppermute | solution.py:49
  29.9 0.8 %collective-permute-start.15 = (bf16[32,1152]{1,0:T(8,128)(2,1)S(1)}, bf16[32,1152]{1,0:T(8,128)(2,1)S(1)}, u32[]{:S(2)}, u32[]{:S(2)}) collective-permute-start(bf16[32,1152]{1,0:T(8,128)(2,1)S(1)} %get-tuple-element.47), channel_id=1, source_target_pairs={{0,2},{1,3},{2,0},{3,1},{4,6},{5,7},{6,4},{7,5},{8,10},{9,11},{10,... | collective-permute-start | bytes 221192 | tf_op jit(solution)/shard_map/ppermute | solution.py:49
  30.7 0.7 %collective-permute-start.16 = (bf16[32,1152]{1,0:T(8,128)(2,1)S(1)}, bf16[32,1152]{1,0:T(8,128)(2,1)S(1)}, u32[]{:S(2)}, u32[]{:S(2)}) collective-permute-start(bf16[32,1152]{1,0:T(8,128)(2,1)S(1)} %get-tuple-element.48), channel_id=1, source_target_pairs={{0,1},{1,0},{2,3},{3,2},{4,5},{5,4},{6,7},{7,6},{8,9},{9,8},{10,11... | collective-permute-start | bytes 221192 | tf_op jit(solution)/shard_map/ppermute | solution.py:49
  31.4 1.5 %collective-permute-start.10 = (bf16[32,1152]{1,0:T(8,128)(2,1)S(1)}, bf16[32,1152]{1,0:T(8,128)(2,1)S(1)}, u32[]{:S(2)}, u32[]{:S(2)}) collective-permute-start(bf16[32,1152]{1,0:T(8,128)(2,1)S(1)} %relay_kernel.1), channel_id=1, source_target_pairs={{0,2},{1,3},{2,0},{3,1},{4,6},{5,7},{6,4},{7,5},{8,10},{9,11},{10,... | collective-permute-start | bytes 221192 | tf_op jit(solution)/shard_map/ppermute | solution.py:49
  33.1 0.9 %collective-permute-done.15.refs_5_ = bf16[32,1152]{1,0:T(8,128)(2,1)S(1)} collective-permute-done((bf16[32,1152]{1,0:T(8,128)(2,1)S(1)}, bf16[32,1152]{1,0:T(8,128)(2,1)S(1)}, u32[]{:S(2)}, u32[]{:S(2)}) %collective-permute-start.15) | collective-permute-done | bytes 73760 | tf_op jit(solution)/shard_map/ppermute | solution.py:49
  33.9 0.8 %collective-permute-done.16.refs_6_ = bf16[32,1152]{1,0:T(8,128)(2,1)S(1)} collective-permute-done((bf16[32,1152]{1,0:T(8,128)(2,1)S(1)}, bf16[32,1152]{1,0:T(8,128)(2,1)S(1)}, u32[]{:S(2)}, u32[]{:S(2)}) %collective-permute-start.16) | collective-permute-done | bytes 73760 | tf_op jit(solution)/shard_map/ppermute | solution.py:49
  34.8 0.5 %total_kernel.1 = (bf16[16,1152]{1,0:T(8,128)(2,1)S(1)}, f32[1,256]{1,0:T(1,128)S(1)}, bf16[32,1152]{1,0:T(8,128)(2,1)S(1)}) custom-call(bf16[256,1152]{1,0:T(8,128)(2,1)S(1)} %bitcast.20, f32[2,1152]{1,0:T(2,128)S(1)} %bitcast.21, f32[6,1,1152]{2,1,0:T(1,128)S(1)} %get-tuple-element.43.refs_2_, f32[32,1152]{1,0:T(8,128)S(1)} %get-tuple-element.45.refs_3_, ...), custom_call_target="tpu_custom_call" | custom-call | tf_op jit(solution)/shard_map/total_kernel/pallas_call | solution.py:64
  35.3 5.2 %collective-permute-start.17 = (bf16[32,1152]{1,0:T(8,128)(2,1)S(1)}, bf16[32,1152]{1,0:T(8,128)(2,1)S(1)}, u32[]{:S(2)}, u32[]{:S(2)}) collective-permute-start(bf16[32,1152]{1,0:T(8,128)(2,1)S(1)} %get-tuple-element.51), channel_id=1, source_target_pairs={{0,16},{16,0},{1,17},{17,1},{2,18},{18,2},{3,19},{19,3},{4,20},{20... | collective-permute-start | bytes 221192 | tf_op jit(solution)/shard_map/ppermute | solution.py:440
  40.5 0.8 %fresh_kernel.1 = bf16[32,2304]{1,0:T(8,128)(2,1)} custom-call(bf16[32,1152]{1,0:T(8,128)(2,1)S(1)} %collective-permute-done.10.refs_0_, bf16[32,1152]{1,0:T(8,128)(2,1)S(1)} %collective-permute-done.9.refs_0_.refs_1_, bf16[32,576]{1,0:T(8,128)(2,1)S(1)} %get-tuple-element.42.refs_2_), custom_call_target="tpu_custom_call" | custom-call | flops 1000000000 | tf_op jit(solution)/shard_map/fresh_kernel/pallas_call | solution.py:64
  41.4 0.6 %final_kernel.1 = (bf16[16,1152]{1,0:T(8,128)(2,1)}, f32[1,256]{1,0:T(1,128)}, f32[1,256]{1,0:T(1,128)}) custom-call(f32[1,256]{1,0:T(1,128)S(1)} %copy-done.1, f32[1,256]{1,0:T(1,128)S(1)} %get-tuple-element.50.refs_1_, bf16[32,1152]{1,0:T(8,128)(2,1)S(1)} %collective-permute-done.17.refs_2_, bf16[16,1152]{1,0:T(8,128)(2,1)S(1)} %get-tuple-element.52.refs_3_, ...), custom_call_target="tpu_custom_call" | custom-call | tf_op jit(solution)/shard_map/final_kernel/pallas_call | solution.py:64
  (30 shorter events, 0.9 us)
Async XLA Ops:
  1.8 7.0 %collective-permute-start = (bf16[40,1152]{1,0:T(8,128)(2,1)S(1)}, bf16[40,1152]{1,0:T(8,128)(2,1)S(1)}, u32[]{:S(2)}, u32[]{:S(2)}) collective-permute-start(bf16[40,1152]{1,0:T(8,128)(2,1)S(1)} %get-tuple-element.30.refs_4_.refs_5_), channel_id=1, source_target_pairs={{0,3},{1,2},{2,1},{3,0},{4,7},{5,6},{6,5},{7,4},{8,11},{9,10},{10,... | collective-permute-start | bytes 276488 | tf_op jit(solution)/shard_map/ppermute | solution.py:49
  4.9 4.2 %collective-permute-start.1 = (bf16[40,1152]{1,0:T(8,128)(2,1)S(1)}, bf16[40,1152]{1,0:T(8,128)(2,1)S(1)}, u32[]{:S(2)}, u32[]{:S(2)}) collective-permute-start(bf16[40,1152]{1,0:T(8,128)(2,1)S(1)} %get-tuple-element.30.refs_4_.refs_5_), channel_id=1, source_target_pairs={{0,2},{1,3},{2,0},{3,1},{4,6},{5,7},{6,4},{7,5},{8,10},{9,11},{10,... | collective-permute-start | bytes 276488 | tf_op jit(solution)/shard_map/ppermute | solution.py:49
  5.1 4.4 %collective-permute-start.2 = (bf16[40,1152]{1,0:T(8,128)(2,1)S(1)}, bf16[40,1152]{1,0:T(8,128)(2,1)S(1)}, u32[]{:S(2)}, u32[]{:S(2)}) collective-permute-start(bf16[40,1152]{1,0:T(8,128)(2,1)S(1)} %get-tuple-element.30.refs_4_.refs_5_), channel_id=1, source_target_pairs={{0,1},{1,0},{2,3},{3,2},{4,5},{5,4},{6,7},{7,6},{8,9},{9,8},{10,11... | collective-permute-start | bytes 276488 | tf_op jit(solution)/shard_map/ppermute | solution.py:49
  5.9 3.6 %copy-start.4 = (bf16[1,1,1152,864]{2,3,1,0:T(8,128)(2,1)S(1)}, bf16[1,1,1152,864]{2,3,1,0:T(8,128)(2,1)}, u32[]{:S(2)}) copy-start(bf16[1,1,1152,864]{2,3,1,0:T(8,128)(2,1)} %param.18) | copy-start | bytes 5971972
  6.2 5.3 %collective-permute-start.3 = (bf16[48,1152]{1,0:T(8,128)(2,1)S(1)}, bf16[48,1152]{1,0:T(8,128)(2,1)S(1)}, u32[]{:S(2)}, u32[]{:S(2)}) collective-permute-start(bf16[48,1152]{1,0:T(8,128)(2,1)S(1)} %get-tuple-element.33), channel_id=1, source_target_pairs={{0,3},{1,2},{2,1},{3,0},{4,7},{5,6},{6,5},{7,4},{8,11},{9,10},{10,... | collective-permute-start | bytes 331784 | tf_op jit(solution)/shard_map/ppermute | solution.py:49
  8.6 5.4 %collective-permute-start.4 = (bf16[48,1152]{1,0:T(8,128)(2,1)S(1)}, bf16[48,1152]{1,0:T(8,128)(2,1)S(1)}, u32[]{:S(2)}, u32[]{:S(2)}) collective-permute-start(bf16[48,1152]{1,0:T(8,128)(2,1)S(1)} %get-tuple-element.34), channel_id=1, source_target_pairs={{0,2},{1,3},{2,0},{3,1},{4,6},{5,7},{6,4},{7,5},{8,10},{9,11},{10,... | collective-permute-start | bytes 331784 | tf_op jit(solution)/shard_map/ppermute | solution.py:49
  8.8 5.2 %collective-permute-start.5 = (bf16[48,1152]{1,0:T(8,128)(2,1)S(1)}, bf16[48,1152]{1,0:T(8,128)(2,1)S(1)}, u32[]{:S(2)}, u32[]{:S(2)}) collective-permute-start(bf16[48,1152]{1,0:T(8,128)(2,1)S(1)} %get-tuple-element.35), channel_id=1, source_target_pairs={{0,1},{1,0},{2,3},{3,2},{4,5},{5,4},{6,7},{7,6},{8,9},{9,8},{10,11... | collective-permute-start | bytes 331784 | tf_op jit(solution)/shard_map/ppermute | solution.py:49
  13.9 6.8 %copy-start.5 = (bf16[1,1,1152,288]{2,3,1,0:T(8,128)(2,1)S(1)}, bf16[1,1,1152,288]{2,3,1,0:T(8,128)(2,1)}, u32[]{:S(2)}) copy-start(bf16[1,1,1152,288]{2,3,1,0:T(8,128)(2,1)} %param.19) | copy-start | bytes 1990660
  14.0 13.1 %copy-start.3 = (bf16[1,1,1152,1152]{3,2,1,0:T(8,128)(2,1)S(1)}, bf16[1,1,1152,1152]{3,2,1,0:T(8,128)(2,1)}, u32[]{:S(2)}) copy-start(bf16[1,1,1152,1152]{3,2,1,0:T(8,128)(2,1)} %param.20) | copy-start | bytes 7962628
  15.3 11.8 %copy-start.2 = (bf16[1,1,1152,1152]{3,2,1,0:T(8,128)(2,1)S(1)}, bf16[1,1,1152,1152]{3,2,1,0:T(8,128)(2,1)}, u32[]{:S(2)}) copy-start(bf16[1,1,1152,1152]{3,2,1,0:T(8,128)(2,1)} %param.21) | copy-start | bytes 7962628
  15.3 4.2 %collective-permute-start.6 = (bf16[32,1152]{1,0:T(8,128)(2,1)S(1)}, bf16[32,1152]{1,0:T(8,128)(2,1)S(1)}, u32[]{:S(2)}, u32[]{:S(2)}) collective-permute-start(bf16[32,1152]{1,0:T(8,128)(2,1)S(1)} %attend_kernel.1.refs_5_), channel_id=1, source_target_pairs={{0,3},{1,2},{2,1},{3,0},{4,7},{5,6},{6,5},{7,4},{8,11},{9,10},{10,... | collective-permute-start | bytes 221192 | tf_op jit(solution)/shard_map/ppermute | solution.py:49
  16.2 4.0 %collective-permute-start.7 = (bf16[32,1152]{1,0:T(8,128)(2,1)S(1)}, bf16[32,1152]{1,0:T(8,128)(2,1)S(1)}, u32[]{:S(2)}, u32[]{:S(2)}) collective-permute-start(bf16[32,1152]{1,0:T(8,128)(2,1)S(1)} %attend_kernel.1.refs_5_), channel_id=1, source_target_pairs={{0,2},{1,3},{2,0},{3,1},{4,6},{5,7},{6,4},{7,5},{8,10},{9,11},{10,... | collective-permute-start | bytes 221192 | tf_op jit(solution)/shard_map/ppermute | solution.py:49
  17.5 3.2 %collective-permute-start.8 = (bf16[32,1152]{1,0:T(8,128)(2,1)S(1)}, bf16[32,1152]{1,0:T(8,128)(2,1)S(1)}, u32[]{:S(2)}, u32[]{:S(2)}) collective-permute-start(bf16[32,1152]{1,0:T(8,128)(2,1)S(1)} %attend_kernel.1.refs_5_), channel_id=1, source_target_pairs={{0,1},{1,0},{2,3},{3,2},{4,5},{5,4},{6,7},{7,6},{8,9},{9,8},{10,11... | collective-permute-start | bytes 221192 | tf_op jit(solution)/shard_map/ppermute | solution.py:49
  21.5 5.2 %collective-permute-start.11 = (bf16[32,1152]{1,0:T(8,128)(2,1)S(1)}, bf16[32,1152]{1,0:T(8,128)(2,1)S(1)}, u32[]{:S(2)}, u32[]{:S(2)}) collective-permute-start(bf16[32,1152]{1,0:T(8,128)(2,1)S(1)} %get-tuple-element.44.refs_9_), channel_id=1, source_target_pairs={{0,3},{1,2},{2,1},{3,0},{4,7},{5,6},{6,5},{7,4},{8,11},{9,10},{10,... | collective-permute-start | bytes 221192 | tf_op jit(solution)/shard_map/ppermute | solution.py:49
  23.9 3.2 %collective-permute-start.12 = (bf16[32,1152]{1,0:T(8,128)(2,1)S(1)}, bf16[32,1152]{1,0:T(8,128)(2,1)S(1)}, u32[]{:S(2)}, u32[]{:S(2)}) collective-permute-start(bf16[32,1152]{1,0:T(8,128)(2,1)S(1)} %get-tuple-element.44.refs_9_), channel_id=1, source_target_pairs={{0,2},{1,3},{2,0},{3,1},{4,6},{5,7},{6,4},{7,5},{8,10},{9,11},{10,... | collective-permute-start | bytes 221192 | tf_op jit(solution)/shard_map/ppermute | solution.py:49
  23.9 3.2 %collective-permute-start.13 = (bf16[32,1152]{1,0:T(8,128)(2,1)S(1)}, bf16[32,1152]{1,0:T(8,128)(2,1)S(1)}, u32[]{:S(2)}, u32[]{:S(2)}) collective-permute-start(bf16[32,1152]{1,0:T(8,128)(2,1)S(1)} %get-tuple-element.44.refs_9_), channel_id=1, source_target_pairs={{0,1},{1,0},{2,3},{3,2},{4,5},{5,4},{6,7},{7,6},{8,9},{9,8},{10,11... | collective-permute-start | bytes 221192 | tf_op jit(solution)/shard_map/ppermute | solution.py:49
  25.5 5.9 %collective-permute-start.9 = (bf16[32,1152]{1,0:T(8,128)(2,1)S(1)}, bf16[32,1152]{1,0:T(8,128)(2,1)S(1)}, u32[]{:S(2)}, u32[]{:S(2)}) collective-permute-start(bf16[32,1152]{1,0:T(8,128)(2,1)S(1)} %get-tuple-element.40), channel_id=1, source_target_pairs={{0,1},{1,0},{2,3},{3,2},{4,5},{5,4},{6,7},{7,6},{8,9},{9,8},{10,11... | collective-permute-start | bytes 221192 | tf_op jit(solution)/shard_map/ppermute | solution.py:49
  28.7 6.0 %copy-start.6 = (bf16[1152,16]{0,1:T(8,128)(2,1)S(1)}, bf16[1152,16]{0,1:T(8,128)(2,1)}, u32[]{:S(2)}) copy-start(bf16[1152,16]{0,1:T(8,128)(2,1)} %param.22) | copy-start | bytes 110596
  28.7 6.1 %copy-start = (f32[1,2,1152]{2,1,0:T(2,128)S(1)}, f32[1,2,1152]{2,1,0:T(2,128)}, u32[]{:S(2)}) copy-start(f32[1,2,1152]{2,1,0:T(2,128)} %param.17) | copy-start | bytes 27652
  28.7 4.4 %collective-permute-start.14 = (bf16[32,1152]{1,0:T(8,128)(2,1)S(1)}, bf16[32,1152]{1,0:T(8,128)(2,1)S(1)}, u32[]{:S(2)}, u32[]{:S(2)}) collective-permute-start(bf16[32,1152]{1,0:T(8,128)(2,1)S(1)} %get-tuple-element.46), channel_id=1, source_target_pairs={{0,3},{1,2},{2,1},{3,0},{4,7},{5,6},{6,5},{7,4},{8,11},{9,10},{10,... | collective-permute-start | bytes 221192 | tf_op jit(solution)/shard_map/ppermute | solution.py:49
  29.9 4.0 %collective-permute-start.15 = (bf16[32,1152]{1,0:T(8,128)(2,1)S(1)}, bf16[32,1152]{1,0:T(8,128)(2,1)S(1)}, u32[]{:S(2)}, u32[]{:S(2)}) collective-permute-start(bf16[32,1152]{1,0:T(8,128)(2,1)S(1)} %get-tuple-element.47), channel_id=1, source_target_pairs={{0,2},{1,3},{2,0},{3,1},{4,6},{5,7},{6,4},{7,5},{8,10},{9,11},{10,... | collective-permute-start | bytes 221192 | tf_op jit(solution)/shard_map/ppermute | solution.py:49
  30.7 4.0 %collective-permute-start.16 = (bf16[32,1152]{1,0:T(8,128)(2,1)S(1)}, bf16[32,1152]{1,0:T(8,128)(2,1)S(1)}, u32[]{:S(2)}, u32[]{:S(2)}) collective-permute-start(bf16[32,1152]{1,0:T(8,128)(2,1)S(1)} %get-tuple-element.48), channel_id=1, source_target_pairs={{0,1},{1,0},{2,3},{3,2},{4,5},{5,4},{6,7},{7,6},{8,9},{9,8},{10,11... | collective-permute-start | bytes 221192 | tf_op jit(solution)/shard_map/ppermute | solution.py:49
  31.4 9.1 %collective-permute-start.10 = (bf16[32,1152]{1,0:T(8,128)(2,1)S(1)}, bf16[32,1152]{1,0:T(8,128)(2,1)S(1)}, u32[]{:S(2)}, u32[]{:S(2)}) collective-permute-start(bf16[32,1152]{1,0:T(8,128)(2,1)S(1)} %relay_kernel.1), channel_id=1, source_target_pairs={{0,2},{1,3},{2,0},{3,1},{4,6},{5,7},{6,4},{7,5},{8,10},{9,11},{10,... | collective-permute-start | bytes 221192 | tf_op jit(solution)/shard_map/ppermute | solution.py:49
  34.7 6.7 %copy-start.1 = (f32[1,256]{1,0:T(1,128)S(1)}, f32[1,256]{1,0:T(1,128)}, u32[]{:S(2)}) copy-start(f32[1,256]{1,0:T(1,128)} %refs_0_.2) | copy-start | bytes 3076
  35.3 6.1 %collective-permute-start.17 = (bf16[32,1152]{1,0:T(8,128)(2,1)S(1)}, bf16[32,1152]{1,0:T(8,128)(2,1)S(1)}, u32[]{:S(2)}, u32[]{:S(2)}) collective-permute-start(bf16[32,1152]{1,0:T(8,128)(2,1)S(1)} %get-tuple-element.51), channel_id=1, source_target_pairs={{0,16},{16,0},{1,17},{17,1},{2,18},{18,2},{3,19},{19,3},{4,20},{20... | collective-permute-start | bytes 221192 | tf_op jit(solution)/shard_map/ppermute | solution.py:440

commit v3 on v2

--- a/solution.py
+++ b/solution.py
@@ -135,7 +135,7 @@
 
 
 def pack_kernel(stale, patch, *rest):
-    *outs, packed = rest
+    outs = rest
     width = stale.shape[1] // 2
     part = width // UNIT_GROUPS
     fresh = 2 * outs[0].shape[0] // 3
@@ -150,14 +150,18 @@
         kept.append(rows)
     keys = [cut(rows[:, :width], UNIT_GROUPS) for rows in kept]
     values = [cut(rows[:, width:], UNIT_GROUPS) for rows in kept]
+    whole = []
     for block in range(UNIT_GROUPS):
-        first = [rows[block] for rows in keys] + [values[0][block]]
         second = beside([rows[block] for rows in values[1:]])
-        packed[block, :fresh, :] = beside(first)
-        packed[block, fresh:, :] = beside([second[: fresh // 2], second[fresh // 2 :]])
+        first = beside([rows[block] for rows in keys] + [values[0][block]])
+        whole.append((first, beside([second[: fresh // 2], second[fresh // 2 :]])))
     here = own_block()
-    for k, out in zip(ORDER, outs):
-        out[...] = packed[other_block(here, k)]
+    for block in range(UNIT_GROUPS):
+
+        @pl.when(here == block)
+        def _():
+            for k, out in zip(ORDER, outs):
+                out[:fresh, :], out[fresh:, :] = whole[block ^ k]
 
 
 def unpack(packed):
@@ -167,7 +171,7 @@
     return first[:3], first[3:] + second
 
 
-def join_kernel(t0, t1, t2, t3, weight, queries, keys, values, near, second, own):
+def join_kernel(t0, t1, t2, t3, p0, weight, queries, keys, values, near, second, own, mixed):
     tokens = []
     for packed in (t0, t1, t2, t3):
         rows = layer_norm(token_rows(packed).astype(F32))
@@ -190,6 +194,8 @@
     near[...] = beside([pairs[1], pairs[3]])
     second[...] = pairs[2]
     own[...] = pairs[0]
+    spread = below([jnp.where(inside[h], q[:fresh], zero) for h in range(heads)])
+    mixed[...] = attention(spread, (p0,), [k[:fresh]], [v[:fresh]])[0]
 
 
 def head_lanes(rows, part):
@@ -199,45 +205,64 @@
     return [(lane >= h * head_size) & (lane < (h + 1) * head_size) for h in range(heads)]
 
 
-def attend_kernel(queries, k, v, p0, p1, p2, p3, sent):
-    count, part = k.shape
-    fresh = count // UNIT_GROUPS
+def attention(queries, packs, fresh_keys, fresh_values):
+    fresh, part = fresh_keys[0].shape
     heads = HEADS // UNIT_GROUPS
+    span = heads * fresh
     inside = head_lanes(fresh, part)
+    stale = [unpack(packed) for packed in packs]
     scores = []
-    values = []
-    for m, packed in enumerate((p0, p1, p2, p3)):
-        rows = slice(m * fresh, (m + 1) * fresh)
-        stale_keys, stale_values = unpack(packed)
-        spread = queries[m * heads * fresh : (m + 1) * heads * fresh, :]
-        scores.append(product(spread, below(stale_keys + [k[rows, :]])))
-        values.append(below(stale_values + [v[rows, :]]))
+    for m, ((stale_keys, _), k) in enumerate(zip(stale, fresh_keys)):
+        scores.append(product(queries[m * span : (m + 1) * span], below(stale_keys + [k])))
     scores = below(scores) * (part // heads) ** (-0.5)
-    raised = jnp.exp(scores - jnp.max(scores, axis=-1, keepdims=True))
-    probs = (raised * (1.0 / jnp.sum(raised, axis=-1, keepdims=True))).astype(BF16)
+    raised = jnp.exp(scores - jnp.max(scores, axis=-1, keepdims=True)).astype(BF16)
+    ones = jnp.ones((scores.shape[1], part // 3), BF16)
     mixed = []
-    for m in range(UNIT_GROUPS):
-        found = jnp.dot(probs[m * heads * fresh : (m + 1) * heads * fresh], values[m], preferred_element_type=F32)
+    for m, ((_, stale_values), v) in enumerate(zip(stale, fresh_values)):
+        rows = beside([below(stale_values + [v]), ones])
+        found = jnp.dot(raised[m * span : (m + 1) * span], rows, preferred_element_type=F32)
+        found = found[:, :part] * (1.0 / found[:, part : part + 1])
         total = jnp.where(inside[0], found[:fresh], 0.0)
         for h in range(1, heads):
             total = jnp.where(inside[h], found[h * fresh : (h + 1) * fresh], total)
         mixed.append(total.astype(BF16))
-    sent[...] = beside(mixed)
+    return mixed
+
+
+def attend_kernel(queries, k, v, own, p1, p2, p3, sent):
+    fresh = own.shape[0]
+    rows = [slice(m * fresh, (m + 1) * fresh) for m in range(1, UNIT_GROUPS)]
+    span = queries.shape[0] // UNIT_GROUPS
+    mixed = attention(queries[span:, :], (p1, p2, p3), [k[row, :] for row in rows], [v[row, :] for row in rows])
+    sent[...] = beside([own[...]] + mixed)
 
 
 def place_blocks(columns, pieces):
     here = own_block()
-    for k, piece in enumerate(pieces):
-        slots = cut(piece[...], UNIT_GROUPS)
-        columns[other_block(here, k)] = below([slots[k ^ m] for m in range(UNIT_GROUPS)])
-    return beside([columns[block] for block in range(UNIT_GROUPS)])
-
-
-def project_kernel(a0, a1, a2, a3, weight, near, sent, onward, columns):
+    fresh, width = pieces[0].shape
+    part = width // UNIT_GROUPS
+    for block in range(UNIT_GROUPS):
+
+        @pl.when(here == block)
+        def _():
+            slots = [cut(piece[...], UNIT_GROUPS) for piece in pieces]
+            for m in range(UNIT_GROUPS):
+                columns[m * fresh : (m + 1) * fresh, :] = beside(
+                    [slots[k][k ^ m] for k in [block ^ other for other in range(UNIT_GROUPS)]]
+                )
+
+    return columns[...]
+
+
+def project_kernel(a0, a1, a2, a3, weight, sent, columns):
     projected = product(place_blocks(columns, (a0, a1, a2, a3)), weight[...]).astype(BF16)
     fresh = sent.shape[0]
-    onward[...] = near[...]
     sent[...] = beside([projected[m * fresh : (m + 1) * fresh] for m in range(UNIT_GROUPS)])
+
+
+def hold_kernel(rows, arrived, out):
+    del arrived
+    out[...] = rows[...]
 
 
 def relay_kernel(second, arrived, onward):
@@ -271,7 +296,8 @@
         out[...] = partial_out[m * fresh : (m + 1) * fresh].astype(BF16)
 
 
-def total_kernel(o0, o1, o2, o3, home, mods, last_mods, weight, kept, noise, sent):
+def total_kernel(o0, o1, o2, o3, home, mods, last_mods, weight, fresh_kv, kept, noise, sent):
+    del fresh_kv
     half = kept.shape[0]
     section = lax.axis_index("section")
     columns = noise.shape[1]
@@ -362,7 +388,6 @@
         [shape((pack_rows, width), BF16)] * UNIT_GROUPS,
         stale,
         patch_index,
-        scratch=[pltpu.VMEM((UNIT_GROUPS, pack_rows, width), BF16)],
         micros=6.0,
     )
     factors = call(
@@ -374,7 +399,7 @@
     )
     packs = swap_each(packs)
     w_qkv = qkv_blocks[0, 0].T
-    queries, keys, values, near, second, own = call(
+    queries, keys, values, near, second, own, mixed = call(
         join_kernel,
         [
             shape((HEADS // UNIT_GROUPS * count, part), BF16),
@@ -383,23 +408,25 @@
             shape((fresh, width), BF16),
             shape((fresh, 2 * part), BF16),
             shape((fresh, 2 * part), BF16),
+            shape((fresh, part), BF16),
         ],
         *slots,
+        packs[0],
         w_qkv,
         micros=1.0,
     )
-    sent = call(attend_kernel, shape((fresh, width), BF16), queries, keys, values, *packs, micros=2.0)
+    sent = call(attend_kernel, shape((fresh, width), BF16), queries, keys, values, mixed, *packs[1:], micros=2.0)
     mixed = [sent] + [swap(sent, k) for k in others]
-    sent, near = call(
+    sent = call(
         project_kernel,
-        [shape((fresh, width), BF16)] * 2,
+        shape((fresh, width), BF16),
         *mixed,
         out_blocks[0, 0].T,
-        near,
-        scratch=[pltpu.VMEM((UNIT_GROUPS, count, part), BF16)],
+        scratch=[pltpu.VMEM((count, width), BF16)],
         micros=1.0,
     )
     pieces = [sent] + [swap(sent, k) for k in others]
+    near = call(hold_kernel, shape((fresh, width), BF16), near, mixed[3], micros=0.1)
     near = swap(near, 1)
     onward = call(relay_kernel, shape((fresh, width), BF16), second, near, micros=0.1)
     fresh_kv = call(
@@ -418,7 +445,7 @@
         *slots,
         up_blocks[0, 0],
         down_blocks[0, 0],
-        scratch=[pltpu.VMEM((UNIT_GROUPS, count, part), BF16)],
+        scratch=[pltpu.VMEM((count, width), BF16)],
         micros=2.0,
     )
     parts = swap_each(parts)
@@ -431,6 +458,8 @@
         mods,
         final_mod[0],
         jnp.tile(final_weight.T, (half, 1)),
+        fresh_kv,
+        far=(8,),
     )
     next_rows, noise, denoised = call(
         final_kernel,

time: 42.7 us -> 42.2 us (0.988)
  starting transfers between devices: 22.2 us -> 20.1 us
  waiting for transfers between devices: 8.79 us -> 10.5 us
    ppermute x17, starting transfers between devices: 17 us -> 15.2 us  [swap(): lax.ppermute(x, 'req', [(i, i ^ k) for i in range(lax.axis_size('req'))])]
    ppermute x17, waiting for transfers between devices: 8.73 us -> 9.67 us  [swap(): lax.ppermute(x, 'req', [(i, i ^ k) for i in range(lax.axis_size('req'))])]
    ppermute x1, waiting for transfers between devices: 0.06 us -> 0.81 us  [per_device(): lax.ppermute(sent, 'section', [(0, 1), (1, 0)])]
    pallas_call x11 -> x12, Pallas kernels: 8.3 us -> 8.28 us  [call(): pl.pallas_call(turned, out_shape=outs, in_specs=specs[::way], out_specs=j...]
  transfers between devices with their start and end apart: 18 -> 18, of which waited for: 11 -> 12; matrix products, arithmetic and copies ran while one was open for 0% -> 0% of each run, Pallas kernels for 11% -> 12%
where the time goes in v3:
time: 42.2 us; the launch traced here: 41.7 us
  starting transfers between devices  20.1 us (48%)
  waiting for transfers between devices  10.5 us (25%)
  Pallas kernels  8.28 us (20%)
  between operations  2.74 us (6%)
    ppermute x17, starting transfers between devices, swap(): lax.ppermute(x, 'req', [(i, i ^ k) for i in range(lax.axis_size('req'))])  15.2 us
    ppermute x17, waiting for transfers between devices, swap(): lax.ppermute(x, 'req', [(i, i ^ k) for i in range(lax.axis_size('req'))])  9.67 us
    pallas_call x12, Pallas kernels, call(): pl.pallas_call(turned, out_shape=outs, in_specs=specs[::way], out_specs=j...  8.28 us
    ppermute x1, starting transfers between devices, per_device(): lax.ppermute(sent, 'section', [(0, 1), (1, 0)])  4.93 us
  transfers between devices with their start and end apart: 18, of which 12 were waited for; matrix products, arithmetic and copies ran while one was open for 0% of the time, Pallas kernels for 12%

profile of v3, /device:TPU:1, one launch (start us, length us, event | category | flops | bytes accessed | tf_op | source)
XLA Modules:
  0.0 41.7 jit_solution(8754756644405904949)
XLA Ops:
  0.6 1.2 %gather_kernel.1 = (bf16[40,1152]{1,0:T(8,128)(2,1)S(1)}, f32[6,1,1152]{2,1,0:T(1,128)S(1)}, bf16[128,2304]{1,0:T(8,128)(2,1)S(1)}) custom-call(bf16[128,2304]{1,0:T(8,128)(2,1)} %bitcast.28, f32[6,1,1152]{2,1,0:T(1,128)} %bitcast.31, bf16[32,1152]{1,0:T(8,128)(2,1)} %bitcast.29), custom_call_target="tpu_custom_call" | custom-call | flops 1000000000 | tf_op jit(solution)/shard_map/gather_kernel/pallas_call | solution.py:64
  1.8 3.1 %collective-permute-start.3 = (bf16[40,1152]{1,0:T(8,128)(2,1)S(1)}, bf16[40,1152]{1,0:T(8,128)(2,1)S(1)}, u32[]{:S(2)}, u32[]{:S(2)}) collective-permute-start(bf16[40,1152]{1,0:T(8,128)(2,1)S(1)} %get-tuple-element.34.refs_5_), channel_id=1, source_target_pairs={{0,3},{1,2},{2,1},{3,0},{4,7},{5,6},{6,5},{7,4},{8,11},{9,10},{10,... | collective-permute-start | bytes 276488 | tf_op jit(solution)/shard_map/ppermute | solution.py:49
  4.9 0.2 collective-permute-start.4
  5.9 0.3 pack_kernel.1
  6.2 2.3 %collective-permute-start = (bf16[48,1152]{1,0:T(8,128)(2,1)S(1)}, bf16[48,1152]{1,0:T(8,128)(2,1)S(1)}, u32[]{:S(2)}, u32[]{:S(2)}) collective-permute-start(bf16[48,1152]{1,0:T(8,128)(2,1)S(1)} %get-tuple-element.30), channel_id=1, source_target_pairs={{0,3},{1,2},{2,1},{3,0},{4,7},{5,6},{6,5},{7,4},{8,11},{9,10},{10,... | collective-permute-start | bytes 331784 | tf_op jit(solution)/shard_map/ppermute | solution.py:49
  8.6 0.2 collective-permute-start.1
  8.9 0.1 collective-permute-done.4.refs_3_
  9.1 0.4 collective-permute-done.5.refs_4_
  9.5 1.6 %join_kernel.1 = (bf16[512,288]{1,0:T(8,128)(2,1)S(1)}, bf16[128,288]{1,0:T(8,128)(2,1)S(1)}, bf16[128,288]{1,0:T(8,128)(2,1)S(1)}, bf16[32,1152]{1,0:T(8,128)(2...) custom-call(bf16[864,1152]{1,0:T(8,128)(2,1)S(1)} %bitcast.24, ...), custom_call_target="tpu_custom_call" | custom-call | flops 1000000000 | tf_op jit(solution)/shard_map/join_kernel/pallas_call | solution.py:64
  11.1 0.4 %collective-permute-done.refs_0_ = bf16[48,1152]{1,0:T(8,128)(2,1)S(1)} collective-permute-done((bf16[48,1152]{1,0:T(8,128)(2,1)S(1)}, bf16[48,1152]{1,0:T(8,128)(2,1)S(1)}, u32[]{:S(2)}, u32[]{:S(2)}) %collective-permute-start) | collective-permute-done | bytes 110624 | tf_op jit(solution)/shard_map/ppermute | solution.py:49
  11.5 2.5 %collective-permute-done.1.refs_1_ = bf16[48,1152]{1,0:T(8,128)(2,1)S(1)} collective-permute-done((bf16[48,1152]{1,0:T(8,128)(2,1)S(1)}, bf16[48,1152]{1,0:T(8,128)(2,1)S(1)}, u32[]{:S(2)}, u32[]{:S(2)}) %collective-permute-start.1) | collective-permute-done | bytes 110624 | tf_op jit(solution)/shard_map/ppermute | solution.py:49
  14.0 1.0 %attend_kernel.1.refs_4_ = bf16[32,1152]{1,0:T(8,128)(2,1)S(1)} custom-call(bf16[48,1152]{1,0:T(8,128)(2,1)S(1)} %collective-permute-done.refs_0_, bf16[48,1152]{1,0:T(8,128)(2,1)S(1)} %collective-permute-done.1.refs_1_, bf16[48,1152]{1,0:T(8,128)(2,1)S(1)} %collective-permute-done.2.refs_2_, bf16[32,288]{1,0:T(8,128)(2,1)S(1)} %get-tuple-element.35.refs_3_, ...), custom_call_target="tpu_custom_call" | custom-call | flops 2000000000 | tf_op jit(solution)/shard_map/attend_kernel/pallas_call | solution.py:64
  15.0 0.9 %collective-permute-start.6 = (bf16[32,1152]{1,0:T(8,128)(2,1)S(1)}, bf16[32,1152]{1,0:T(8,128)(2,1)S(1)}, u32[]{:S(2)}, u32[]{:S(2)}) collective-permute-start(bf16[32,1152]{1,0:T(8,128)(2,1)S(1)} %attend_kernel.1.refs_4_), channel_id=1, source_target_pairs={{0,3},{1,2},{2,1},{3,0},{4,7},{5,6},{6,5},{7,4},{8,11},{9,10},{10,... | collective-permute-start | bytes 221192 | tf_op jit(solution)/shard_map/ppermute | solution.py:49
  15.9 1.6 %collective-permute-start.10 = (bf16[32,1152]{1,0:T(8,128)(2,1)S(1)}, bf16[32,1152]{1,0:T(8,128)(2,1)S(1)}, u32[]{:S(2)}, u32[]{:S(2)}) collective-permute-start(bf16[32,1152]{1,0:T(8,128)(2,1)S(1)} %attend_kernel.1.refs_4_), channel_id=1, source_target_pairs={{0,1},{1,0},{2,3},{3,2},{4,5},{5,4},{6,7},{7,6},{8,9},{9,8},{10,11... | collective-permute-start | bytes 221192 | tf_op jit(solution)/shard_map/ppermute | solution.py:49
  17.5 0.2 collective-permute-start.9
  17.7 1.5 %collective-permute-done.6.refs_0_.refs_1_ = bf16[32,1152]{1,0:T(8,128)(2,1)S(1)} collective-permute-done((bf16[32,1152]{1,0:T(8,128)(2,1)S(1)}, bf16[32,1152]{1,0:T(8,128)(2,1)S(1)}, u32[]{:S(2)}, u32[]{:S(2)}) %collective-permute-start.6) | collective-permute-done | bytes 73760 | tf_op jit(solution)/shard_map/ppermute | solution.py:49
  19.2 0.8 %collective-permute-start.7 = (bf16[32,1152]{1,0:T(8,128)(2,1)S(1)}, bf16[32,1152]{1,0:T(8,128)(2,1)S(1)}, u32[]{:S(2)}, u32[]{:S(2)}) collective-permute-start(bf16[32,1152]{1,0:T(8,128)(2,1)S(1)} %hold_kernel.1), channel_id=1, source_target_pairs={{0,1},{1,0},{2,3},{3,2},{4,5},{5,4},{6,7},{7,6},{8,9},{9,8},{10,11... | collective-permute-start | bytes 221192 | tf_op jit(solution)/shard_map/ppermute | solution.py:49
  20.1 1.8 %collective-permute-done.9.refs_2_ = bf16[32,1152]{1,0:T(8,128)(2,1)S(1)} collective-permute-done((bf16[32,1152]{1,0:T(8,128)(2,1)S(1)}, bf16[32,1152]{1,0:T(8,128)(2,1)S(1)}, u32[]{:S(2)}, u32[]{:S(2)}) %collective-permute-start.9) | collective-permute-done | bytes 73760 | tf_op jit(solution)/shard_map/ppermute | solution.py:49
  21.8 0.6 %project_kernel.1.refs_9_ = bf16[32,1152]{1,0:T(8,128)(2,1)S(1)} custom-call(bf16[288,1152]{1,0:T(8,128)(2,1)S(1)} %bitcast.25, bf16[32,1152]{1,0:T(8,128)(2,1)S(1)} %collective-permute-done.6.refs_0_.refs_1_, bf16[32,1152]{1,0:T(8,128)(2,1)S(1)} %collective-permute-done.9.refs_2_, bf16[32,1152]{1,0:T(8,128)(2,1)S(1)} %collective-permute-done.10.refs_3_, ...), custom_call_target="tpu_custom_call" | custom-call | flops 1000000000 | tf_op jit(solution)/shard_map/project_kernel/pallas_call | solution.py:64
  22.6 2.5 %collective-permute-start.13 = (bf16[32,1152]{1,0:T(8,128)(2,1)S(1)}, bf16[32,1152]{1,0:T(8,128)(2,1)S(1)}, u32[]{:S(2)}, u32[]{:S(2)}) collective-permute-start(bf16[32,1152]{1,0:T(8,128)(2,1)S(1)} %project_kernel.1.refs_9_), channel_id=1, source_target_pairs={{0,1},{1,0},{2,3},{3,2},{4,5},{5,4},{6,7},{7,6},{8,9},{9,8},{10,11... | collective-permute-start | bytes 221192 | tf_op jit(solution)/shard_map/ppermute | solution.py:49
  26.6 0.8 %collective-permute-done.11.refs_6_ = bf16[32,1152]{1,0:T(8,128)(2,1)S(1)} collective-permute-done((bf16[32,1152]{1,0:T(8,128)(2,1)S(1)}, bf16[32,1152]{1,0:T(8,128)(2,1)S(1)}, u32[]{:S(2)}, u32[]{:S(2)}) %collective-permute-start.11) | collective-permute-done | bytes 73760 | tf_op jit(solution)/shard_map/ppermute | solution.py:49
  27.4 1.5 %mlp_kernel.1 = (bf16[32,1152]{1,0:T(8,128)(2,1)S(1)}, bf16[32,1152]{1,0:T(8,128)(2,1)S(1)}, bf16[32,1152]{1,0:T(8,128)(2,1)S(1)}, bf16[32,1152]{1,0:T(8,128)(2,1)S(1)}, f32[32,1152]{1,0:T(8,128)S(1)}) custom-call(bf16[1152,1152]{1,0:T(8,128)(2,1)S(1)} %bitcast.22, bf16[1152,1152]{1,0:T(8,128)(2,1)S(1)} %bitcast.23, ...), custom_call_target="tpu_custom_call" | custom-call | flops 2000000000 | tf_op jit(solution)/shard_map/mlp_kernel/pallas_call | solution.py:64
  28.9 0.8 %collective-permute-start.14 = (bf16[32,1152]{1,0:T(8,128)(2,1)S(1)}, bf16[32,1152]{1,0:T(8,128)(2,1)S(1)}, u32[]{:S(2)}, u32[]{:S(2)}) collective-permute-start(bf16[32,1152]{1,0:T(8,128)(2,1)S(1)} %get-tuple-element.44), channel_id=1, source_target_pairs={{0,3},{1,2},{2,1},{3,0},{4,7},{5,6},{6,5},{7,4},{8,11},{9,10},{10,... | collective-permute-start | bytes 221192 | tf_op jit(solution)/shard_map/ppermute | solution.py:49
  29.7 1.4 %collective-permute-start.15 = (bf16[32,1152]{1,0:T(8,128)(2,1)S(1)}, bf16[32,1152]{1,0:T(8,128)(2,1)S(1)}, u32[]{:S(2)}, u32[]{:S(2)}) collective-permute-start(bf16[32,1152]{1,0:T(8,128)(2,1)S(1)} %get-tuple-element.45), channel_id=1, source_target_pairs={{0,2},{1,3},{2,0},{3,1},{4,6},{5,7},{6,4},{7,5},{8,10},{9,11},{10,... | collective-permute-start | bytes 221192 | tf_op jit(solution)/shard_map/ppermute | solution.py:49
  31.1 0.5 %collective-permute-start.16 = (bf16[32,1152]{1,0:T(8,128)(2,1)S(1)}, bf16[32,1152]{1,0:T(8,128)(2,1)S(1)}, u32[]{:S(2)}, u32[]{:S(2)}) collective-permute-start(bf16[32,1152]{1,0:T(8,128)(2,1)S(1)} %get-tuple-element.46), channel_id=1, source_target_pairs={{0,1},{1,0},{2,3},{3,2},{4,5},{5,4},{6,7},{7,6},{8,9},{9,8},{10,11... | collective-permute-start | bytes 221192 | tf_op jit(solution)/shard_map/ppermute | solution.py:49
  31.6 0.8 %fresh_kernel.1.refs_0_ = bf16[32,2304]{1,0:T(8,128)(2,1)} custom-call(bf16[32,1152]{1,0:T(8,128)(2,1)S(1)} %collective-permute-done.8.refs_0_, bf16[32,1152]{1,0:T(8,128)(2,1)S(1)} %collective-permute-done.7.refs_0_.refs_1_, bf16[32,576]{1,0:T(8,128)(2,1)S(1)} %get-tuple-element.41.refs_2_), custom_call_target="tpu_custom_call" | custom-call | flops 1000000000 | tf_op jit(solution)/shard_map/fresh_kernel/pallas_call | solution.py:64
  32.5 0.7 %collective-permute-done.14.refs_5_ = bf16[32,1152]{1,0:T(8,128)(2,1)S(1)} collective-permute-done((bf16[32,1152]{1,0:T(8,128)(2,1)S(1)}, bf16[32,1152]{1,0:T(8,128)(2,1)S(1)}, u32[]{:S(2)}, u32[]{:S(2)}) %collective-permute-start.14) | collective-permute-done | bytes 73760 | tf_op jit(solution)/shard_map/ppermute | solution.py:49
  33.2 1.3 %collective-permute-done.15.refs_6_ = bf16[32,1152]{1,0:T(8,128)(2,1)S(1)} collective-permute-done((bf16[32,1152]{1,0:T(8,128)(2,1)S(1)}, bf16[32,1152]{1,0:T(8,128)(2,1)S(1)}, u32[]{:S(2)}, u32[]{:S(2)}) %collective-permute-start.15) | collective-permute-done | bytes 73760 | tf_op jit(solution)/shard_map/ppermute | solution.py:49
  34.7 0.5 %total_kernel.1 = (bf16[16,1152]{1,0:T(8,128)(2,1)S(1)}, f32[1,256]{1,0:T(1,128)S(1)}, bf16[32,1152]{1,0:T(8,128)(2,1)S(1)}) custom-call(bf16[32,2304]{1,0:T(8,128)(2,1)} %fresh_kernel.1.refs_0_, bf16[256,1152]{1,0:T(8,128)(2,1)S(1)} %bitcast.20, f32[2,1152]{1,0:T(2,128)S(1)} %bitcast.21, f32[6,1,1152]{2,1,0:T(1,128)S(1)} %get-tuple-element.42.refs_3_, ...), custom_call_target="tpu_custom_call" | custom-call | tf_op jit(solution)/shard_map/total_kernel/pallas_call | solution.py:64
  35.2 4.9 %collective-permute-start.17 = (bf16[32,1152]{1,0:T(8,128)(2,1)S(1)}, bf16[32,1152]{1,0:T(8,128)(2,1)S(1)}, u32[]{:S(2)}, u32[]{:S(2)}) collective-permute-start(bf16[32,1152]{1,0:T(8,128)(2,1)S(1)} %get-tuple-element.49), channel_id=1, source_target_pairs={{0,16},{16,0},{1,17},{17,1},{2,18},{18,2},{3,19},{19,3},{4,20},{20... | collective-permute-start | bytes 221192 | tf_op jit(solution)/shard_map/ppermute | solution.py:469
  40.2 0.8 %collective-permute-done.17.refs_2_ = bf16[32,1152]{1,0:T(8,128)(2,1)S(1)} collective-permute-done((bf16[32,1152]{1,0:T(8,128)(2,1)S(1)}, bf16[32,1152]{1,0:T(8,128)(2,1)S(1)}, u32[]{:S(2)}, u32[]{:S(2)}) %collective-permute-start.17) | collective-permute-done | bytes 73760 | tf_op jit(solution)/shard_map/ppermute | solution.py:469
  41.1 0.6 %final_kernel.1 = (bf16[16,1152]{1,0:T(8,128)(2,1)}, f32[1,256]{1,0:T(1,128)}, f32[1,256]{1,0:T(1,128)}) custom-call(f32[1,256]{1,0:T(1,128)S(1)} %copy-done.1, f32[1,256]{1,0:T(1,128)S(1)} %get-tuple-element.48.refs_1_, bf16[32,1152]{1,0:T(8,128)(2,1)S(1)} %collective-permute-done.17.refs_2_, bf16[16,1152]{1,0:T(8,128)(2,1)S(1)} %get-tuple-element.50.refs_3_, ...), custom_call_target="tpu_custom_call" | custom-call | tf_op jit(solution)/shard_map/final_kernel/pallas_call | solution.py:64
  (31 shorter events, 0.9 us)
Async XLA Ops:
  1.8 7.0 %collective-permute-start.3 = (bf16[40,1152]{1,0:T(8,128)(2,1)S(1)}, bf16[40,1152]{1,0:T(8,128)(2,1)S(1)}, u32[]{:S(2)}, u32[]{:S(2)}) collective-permute-start(bf16[40,1152]{1,0:T(8,128)(2,1)S(1)} %get-tuple-element.34.refs_5_), channel_id=1, source_target_pairs={{0,3},{1,2},{2,1},{3,0},{4,7},{5,6},{6,5},{7,4},{8,11},{9,10},{10,... | collective-permute-start | bytes 276488 | tf_op jit(solution)/shard_map/ppermute | solution.py:49
  4.9 4.2 %collective-permute-start.4 = (bf16[40,1152]{1,0:T(8,128)(2,1)S(1)}, bf16[40,1152]{1,0:T(8,128)(2,1)S(1)}, u32[]{:S(2)}, u32[]{:S(2)}) collective-permute-start(bf16[40,1152]{1,0:T(8,128)(2,1)S(1)} %get-tuple-element.34.refs_5_), channel_id=1, source_target_pairs={{0,2},{1,3},{2,0},{3,1},{4,6},{5,7},{6,4},{7,5},{8,10},{9,11},{10,... | collective-permute-start | bytes 276488 | tf_op jit(solution)/shard_map/ppermute | solution.py:49
  5.1 4.4 %collective-permute-start.5 = (bf16[40,1152]{1,0:T(8,128)(2,1)S(1)}, bf16[40,1152]{1,0:T(8,128)(2,1)S(1)}, u32[]{:S(2)}, u32[]{:S(2)}) collective-permute-start(bf16[40,1152]{1,0:T(8,128)(2,1)S(1)} %get-tuple-element.34.refs_5_), channel_id=1, source_target_pairs={{0,1},{1,0},{2,3},{3,2},{4,5},{5,4},{6,7},{7,6},{8,9},{9,8},{10,11... | collective-permute-start | bytes 276488 | tf_op jit(solution)/shard_map/ppermute | solution.py:49
  5.9 3.6 %copy-start.4 = (bf16[1,1,1152,864]{2,3,1,0:T(8,128)(2,1)S(1)}, bf16[1,1,1152,864]{2,3,1,0:T(8,128)(2,1)}, u32[]{:S(2)}) copy-start(bf16[1,1,1152,864]{2,3,1,0:T(8,128)(2,1)} %param.18) | copy-start | bytes 5971972
  6.2 5.3 %collective-permute-start = (bf16[48,1152]{1,0:T(8,128)(2,1)S(1)}, bf16[48,1152]{1,0:T(8,128)(2,1)S(1)}, u32[]{:S(2)}, u32[]{:S(2)}) collective-permute-start(bf16[48,1152]{1,0:T(8,128)(2,1)S(1)} %get-tuple-element.30), channel_id=1, source_target_pairs={{0,3},{1,2},{2,1},{3,0},{4,7},{5,6},{6,5},{7,4},{8,11},{9,10},{10,... | collective-permute-start | bytes 331784 | tf_op jit(solution)/shard_map/ppermute | solution.py:49
  8.6 5.4 %collective-permute-start.1 = (bf16[48,1152]{1,0:T(8,128)(2,1)S(1)}, bf16[48,1152]{1,0:T(8,128)(2,1)S(1)}, u32[]{:S(2)}, u32[]{:S(2)}) collective-permute-start(bf16[48,1152]{1,0:T(8,128)(2,1)S(1)} %get-tuple-element.31), channel_id=1, source_target_pairs={{0,2},{1,3},{2,0},{3,1},{4,6},{5,7},{6,4},{7,5},{8,10},{9,11},{10,... | collective-permute-start | bytes 331784 | tf_op jit(solution)/shard_map/ppermute | solution.py:49
  8.8 5.2 %collective-permute-start.2 = (bf16[48,1152]{1,0:T(8,128)(2,1)S(1)}, bf16[48,1152]{1,0:T(8,128)(2,1)S(1)}, u32[]{:S(2)}, u32[]{:S(2)}) collective-permute-start(bf16[48,1152]{1,0:T(8,128)(2,1)S(1)} %get-tuple-element.32), channel_id=1, source_target_pairs={{0,1},{1,0},{2,3},{3,2},{4,5},{5,4},{6,7},{7,6},{8,9},{9,8},{10,11... | collective-permute-start | bytes 331784 | tf_op jit(solution)/shard_map/ppermute | solution.py:49
  14.0 7.8 %copy-start.5 = (bf16[1,1,1152,288]{2,3,1,0:T(8,128)(2,1)S(1)}, bf16[1,1,1152,288]{2,3,1,0:T(8,128)(2,1)}, u32[]{:S(2)}) copy-start(bf16[1,1,1152,288]{2,3,1,0:T(8,128)(2,1)} %param.19) | copy-start | bytes 1990660
  14.0 13.4 %copy-start.3 = (bf16[1,1,1152,1152]{3,2,1,0:T(8,128)(2,1)S(1)}, bf16[1,1,1152,1152]{3,2,1,0:T(8,128)(2,1)}, u32[]{:S(2)}) copy-start(bf16[1,1,1152,1152]{3,2,1,0:T(8,128)(2,1)} %param.20) | copy-start | bytes 7962628
  15.0 12.4 %copy-start.2 = (bf16[1,1,1152,1152]{3,2,1,0:T(8,128)(2,1)S(1)}, bf16[1,1,1152,1152]{3,2,1,0:T(8,128)(2,1)}, u32[]{:S(2)}) copy-start(bf16[1,1,1152,1152]{3,2,1,0:T(8,128)(2,1)} %param.21) | copy-start | bytes 7962628
  15.0 4.2 %collective-permute-start.6 = (bf16[32,1152]{1,0:T(8,128)(2,1)S(1)}, bf16[32,1152]{1,0:T(8,128)(2,1)S(1)}, u32[]{:S(2)}, u32[]{:S(2)}) collective-permute-start(bf16[32,1152]{1,0:T(8,128)(2,1)S(1)} %attend_kernel.1.refs_4_), channel_id=1, source_target_pairs={{0,3},{1,2},{2,1},{3,0},{4,7},{5,6},{6,5},{7,4},{8,11},{9,10},{10,... | collective-permute-start | bytes 221192 | tf_op jit(solution)/shard_map/ppermute | solution.py:49
  15.9 4.2 %collective-permute-start.10 = (bf16[32,1152]{1,0:T(8,128)(2,1)S(1)}, bf16[32,1152]{1,0:T(8,128)(2,1)S(1)}, u32[]{:S(2)}, u32[]{:S(2)}) collective-permute-start(bf16[32,1152]{1,0:T(8,128)(2,1)S(1)} %attend_kernel.1.refs_4_), channel_id=1, source_target_pairs={{0,1},{1,0},{2,3},{3,2},{4,5},{5,4},{6,7},{7,6},{8,9},{9,8},{10,11... | collective-permute-start | bytes 221192 | tf_op jit(solution)/shard_map/ppermute | solution.py:49
  17.5 4.3 %collective-permute-start.9 = (bf16[32,1152]{1,0:T(8,128)(2,1)S(1)}, bf16[32,1152]{1,0:T(8,128)(2,1)S(1)}, u32[]{:S(2)}, u32[]{:S(2)}) collective-permute-start(bf16[32,1152]{1,0:T(8,128)(2,1)S(1)} %attend_kernel.1.refs_4_), channel_id=1, source_target_pairs={{0,2},{1,3},{2,0},{3,1},{4,6},{5,7},{6,4},{7,5},{8,10},{9,11},{10,... | collective-permute-start | bytes 221192 | tf_op jit(solution)/shard_map/ppermute | solution.py:49
  19.2 7.3 %collective-permute-start.7 = (bf16[32,1152]{1,0:T(8,128)(2,1)S(1)}, bf16[32,1152]{1,0:T(8,128)(2,1)S(1)}, u32[]{:S(2)}, u32[]{:S(2)}) collective-permute-start(bf16[32,1152]{1,0:T(8,128)(2,1)S(1)} %hold_kernel.1), channel_id=1, source_target_pairs={{0,1},{1,0},{2,3},{3,2},{4,5},{5,4},{6,7},{7,6},{8,9},{9,8},{10,11... | collective-permute-start | bytes 221192 | tf_op jit(solution)/shard_map/ppermute | solution.py:49
  22.4 4.9 %collective-permute-start.11 = (bf16[32,1152]{1,0:T(8,128)(2,1)S(1)}, bf16[32,1152]{1,0:T(8,128)(2,1)S(1)}, u32[]{:S(2)}, u32[]{:S(2)}) collective-permute-start(bf16[32,1152]{1,0:T(8,128)(2,1)S(1)} %project_kernel.1.refs_9_), channel_id=1, source_target_pairs={{0,3},{1,2},{2,1},{3,0},{4,7},{5,6},{6,5},{7,4},{8,11},{9,10},{10,... | collective-permute-start | bytes 221192 | tf_op jit(solution)/shard_map/ppermute | solution.py:49
  22.5 4.8 %collective-permute-start.12 = (bf16[32,1152]{1,0:T(8,128)(2,1)S(1)}, bf16[32,1152]{1,0:T(8,128)(2,1)S(1)}, u32[]{:S(2)}, u32[]{:S(2)}) collective-permute-start(bf16[32,1152]{1,0:T(8,128)(2,1)S(1)} %project_kernel.1.refs_9_), channel_id=1, source_target_pairs={{0,2},{1,3},{2,0},{3,1},{4,6},{5,7},{6,4},{7,5},{8,10},{9,11},{10,... | collective-permute-start | bytes 221192 | tf_op jit(solution)/shard_map/ppermute | solution.py:49
  22.6 4.7 %collective-permute-start.13 = (bf16[32,1152]{1,0:T(8,128)(2,1)S(1)}, bf16[32,1152]{1,0:T(8,128)(2,1)S(1)}, u32[]{:S(2)}, u32[]{:S(2)}) collective-permute-start(bf16[32,1152]{1,0:T(8,128)(2,1)S(1)} %project_kernel.1.refs_9_), channel_id=1, source_target_pairs={{0,1},{1,0},{2,3},{3,2},{4,5},{5,4},{6,7},{7,6},{8,9},{9,8},{10,11... | collective-permute-start | bytes 221192 | tf_op jit(solution)/shard_map/ppermute | solution.py:49
  26.5 5.1 %collective-permute-start.8 = (bf16[32,1152]{1,0:T(8,128)(2,1)S(1)}, bf16[32,1152]{1,0:T(8,128)(2,1)S(1)}, u32[]{:S(2)}, u32[]{:S(2)}) collective-permute-start(bf16[32,1152]{1,0:T(8,128)(2,1)S(1)} %relay_kernel.1), channel_id=1, source_target_pairs={{0,2},{1,3},{2,0},{3,1},{4,6},{5,7},{6,4},{7,5},{8,10},{9,11},{10,... | collective-permute-start | bytes 221192 | tf_op jit(solution)/shard_map/ppermute | solution.py:49
  28.9 5.8 %copy-start.6 = (bf16[1152,16]{0,1:T(8,128)(2,1)S(1)}, bf16[1152,16]{0,1:T(8,128)(2,1)}, u32[]{:S(2)}) copy-start(bf16[1152,16]{0,1:T(8,128)(2,1)} %param.22) | copy-start | bytes 110596
  28.9 5.8 %copy-start = (f32[1,2,1152]{2,1,0:T(2,128)S(1)}, f32[1,2,1152]{2,1,0:T(2,128)}, u32[]{:S(2)}) copy-start(f32[1,2,1152]{2,1,0:T(2,128)} %param.17) | copy-start | bytes 27652
  28.9 4.3 %collective-permute-start.14 = (bf16[32,1152]{1,0:T(8,128)(2,1)S(1)}, bf16[32,1152]{1,0:T(8,128)(2,1)S(1)}, u32[]{:S(2)}, u32[]{:S(2)}) collective-permute-start(bf16[32,1152]{1,0:T(8,128)(2,1)S(1)} %get-tuple-element.44), channel_id=1, source_target_pairs={{0,3},{1,2},{2,1},{3,0},{4,7},{5,6},{6,5},{7,4},{8,11},{9,10},{10,... | collective-permute-start | bytes 221192 | tf_op jit(solution)/shard_map/ppermute | solution.py:49
  29.7 4.8 %collective-permute-start.15 = (bf16[32,1152]{1,0:T(8,128)(2,1)S(1)}, bf16[32,1152]{1,0:T(8,128)(2,1)S(1)}, u32[]{:S(2)}, u32[]{:S(2)}) collective-permute-start(bf16[32,1152]{1,0:T(8,128)(2,1)S(1)} %get-tuple-element.45), channel_id=1, source_target_pairs={{0,2},{1,3},{2,0},{3,1},{4,6},{5,7},{6,4},{7,5},{8,10},{9,11},{10,... | collective-permute-start | bytes 221192 | tf_op jit(solution)/shard_map/ppermute | solution.py:49
  31.1 3.5 %collective-permute-start.16 = (bf16[32,1152]{1,0:T(8,128)(2,1)S(1)}, bf16[32,1152]{1,0:T(8,128)(2,1)S(1)}, u32[]{:S(2)}, u32[]{:S(2)}) collective-permute-start(bf16[32,1152]{1,0:T(8,128)(2,1)S(1)} %get-tuple-element.46), channel_id=1, source_target_pairs={{0,1},{1,0},{2,3},{3,2},{4,5},{5,4},{6,7},{7,6},{8,9},{9,8},{10,11... | collective-permute-start | bytes 221192 | tf_op jit(solution)/shard_map/ppermute | solution.py:49
  34.6 6.4 %copy-start.1 = (f32[1,256]{1,0:T(1,128)S(1)}, f32[1,256]{1,0:T(1,128)}, u32[]{:S(2)}) copy-start(f32[1,256]{1,0:T(1,128)} %refs_0_.2) | copy-start | bytes 3076
  35.2 5.8 %collective-permute-start.17 = (bf16[32,1152]{1,0:T(8,128)(2,1)S(1)}, bf16[32,1152]{1,0:T(8,128)(2,1)S(1)}, u32[]{:S(2)}, u32[]{:S(2)}) collective-permute-start(bf16[32,1152]{1,0:T(8,128)(2,1)S(1)} %get-tuple-element.49), channel_id=1, source_target_pairs={{0,16},{16,0},{1,17},{17,1},{2,18},{18,2},{3,19},{19,3},{4,20},{20... | collective-permute-start | bytes 221192 | tf_op jit(solution)/shard_map/ppermute | solution.py:469
